TPU v7x, 32 devices: a whole 2x2x4 slice. The times are simulated.
32 devices in a mesh: grp: 2 (over y), row: 8 (over z, x), col: 2 (over core).
Axes of the slice: x: 2, y: 2, z: 4, core: 2. Of those that a mesh axis runs over, the one named last changes fastest.
Arguments:
- features: bfloat16 [128, 128, 256], P(('grp', 'row'), 'col'), parts along dimension 0, may hold values from -6 to 6
- cotangent: bfloat16 [128, 128, 256], P(('grp', 'row'), 'col'), parts along dimension 0, may hold values from -6 to 6
- domain: int32 [128, 128], P(('grp', 'row'), 'col'), parts along dimension 0, may hold values 0 or 1
- qkv_weight: bfloat16 [256, 768], replicated, may hold values from -6 to 6
- proj_weight: bfloat16 [256, 256], replicated, may hold values from -0.375 to 0.375
- norm_gain: float32 [256], replicated, may hold values from 0.5 to 1.5
Outputs:
- updated: bfloat16 [128, 128, 256], P(('grp', 'row'), 'col'), parts along dimension 0
- grad_features: bfloat16 [128, 128, 256], P(('grp', 'row'), 'col'), parts along dimension 0
- grad_qkv: float32 [512, 768], P('grp'), parts along dimension 0
- grad_proj: float32 [512, 256], P('grp'), parts along dimension 0
- grad_gain: float32 [512], P('grp'), parts along dimension 0
There are 2 independent parts, one for each index of `grp`. A program takes and returns all parts, laid end to end along the dimension named above; an argument that names none is the same for every part. Nothing has to cross between parts.
All inputs are finite; a program needn't handle non-finite values. No bound on the sum of `domain` on one device may be relied on, other than what follows from the above.
Results may differ from a plain program's by a relative error of at most 0.013.
Values may be sent and summed in bfloat16 or wider, within the bound.
A program may use at most 64 MiB of HBM per device.

v0:
```python
import jax
import jax.numpy as jnp
from jax import lax
from jax.sharding import PartitionSpec as P

HEADS = 8
WIN = 8
SHIFT = 4


NORM_EPSILON = 1e-05
MASKED_SCORE = -1e30


def from_behind(array, axis, by):
    peers = lax.axis_size(axis)
    return lax.ppermute(array, axis, [(i, (i + by) % peers) for i in range(peers)])


def layer_norm(values, norm_gain):
    average = jnp.mean(values, -1, keepdims=True)
    centred = values - average
    variance = jnp.mean(centred * centred, -1, keepdims=True)
    return centred * lax.rsqrt(variance + NORM_EPSILON) * norm_gain


def region_of(cell_ids, extent):
    return (cell_ids >= extent - WIN).astype(jnp.int32) + (cell_ids >= extent - SHIFT).astype(
        jnp.int32
    )


def region_labels(row_start, tile_rows, total_rows, col_start, tile_cols, total_cols):
    row_ids = row_start + jnp.arange(tile_rows, dtype=jnp.int32)
    col_ids = col_start + jnp.arange(tile_cols, dtype=jnp.int32)
    return region_of(row_ids, total_rows)[:, None] * 3 + region_of(col_ids, total_cols)[None, :]


def contract_rows(left, right):
    return lax.dot_general(
        left, right, (((0,), (0,)), ((), ())), preferred_element_type=jnp.float32
    )


def contract_cols(left, right):
    return lax.dot_general(
        left, right, (((1,), (1,)), ((), ())), preferred_element_type=jnp.float32
    )


def window_core(projected, labels):
    tile_rows, tile_cols, triple = projected.shape
    channels = triple // 3
    windows = tile_cols // WIN
    head_dim = channels // HEADS
    grouped = (
        projected.reshape(tile_rows, windows, WIN, triple)
        .transpose(1, 0, 2, 3)
        .reshape(windows, tile_rows * WIN, triple)
    )
    grouped_labels = (
        labels.reshape(tile_rows, windows, WIN).transpose(1, 0, 2).reshape(windows, tile_rows * WIN)
    )
    query_part = grouped[:, :, :channels].reshape(windows, -1, HEADS, head_dim)
    key_part = grouped[:, :, channels : 2 * channels].reshape(windows, -1, HEADS, head_dim)
    value_part = grouped[:, :, 2 * channels :].reshape(windows, -1, HEADS, head_dim)
    scores = jnp.einsum("wqhd,wkhd->whqk", query_part, key_part) * head_dim ** (-0.5)
    allowed = (grouped_labels[:, :, None] == grouped_labels[:, None, :])[:, None]
    scores = jnp.where(allowed, scores, MASKED_SCORE)
    peak = lax.stop_gradient(jnp.max(scores, -1, keepdims=True))
    weights = jnp.exp(scores - peak)
    probability = weights / jnp.sum(weights, -1, keepdims=True)
    probability = lax.optimization_barrier(probability.astype(jnp.bfloat16)).astype(jnp.float32)
    context = jnp.einsum("whqk,wkhd->wqhd", probability, value_part)
    context = (
        context.reshape(windows, tile_rows, WIN, channels)
        .transpose(1, 0, 2, 3)
        .reshape(tile_rows, tile_cols, channels)
    )
    return context.astype(jnp.bfloat16)


def forward_block(shifted, labels, qkv_weight, proj_weight):
    tile_rows, tile_cols, channels = shifted.shape
    flat_rows = shifted.reshape(-1, channels)
    projected = jnp.dot(flat_rows, qkv_weight, preferred_element_type=jnp.float32).astype(
        jnp.bfloat16
    )
    projected = projected.reshape(tile_rows, tile_cols, 3 * channels)
    context = window_core(projected.astype(jnp.float32), labels)
    attended = jnp.dot(
        context.reshape(-1, channels), proj_weight, preferred_element_type=jnp.float32
    ).astype(jnp.bfloat16)
    return (projected, context, attended.reshape(shifted.shape))


def backward_block(shifted, labels, projected, context, dattended, qkv_weight, proj_weight):
    channels = shifted.shape[-1]
    grad_rows = dattended.reshape(-1, channels)
    grad_proj = contract_rows(context.reshape(-1, channels), grad_rows)
    dcontext = contract_cols(grad_rows, proj_weight).astype(jnp.bfloat16).reshape(context.shape)

    def core_only(values):
        return window_core(values, labels)

    _, pullback = jax.vjp(core_only, projected.astype(jnp.float32))
    dprojected = pullback(dcontext)[0].astype(jnp.bfloat16).reshape(-1, 3 * channels)
    grad_qkv = contract_rows(shifted.reshape(-1, channels), dprojected)
    dshifted = contract_cols(dprojected, qkv_weight).astype(jnp.bfloat16).reshape(shifted.shape)
    return (grad_qkv, grad_proj, dshifted)


def norm_backward(values, norm_gain, dnormed):

    def apply_norm(inputs):
        return layer_norm(inputs, norm_gain)

    _, pullback = jax.vjp(apply_norm, values)
    upstream = dnormed.astype(jnp.float32)
    grad_values = pullback(upstream)[0]
    standard = layer_norm(values, jnp.ones_like(norm_gain))
    grad_gain = jnp.sum((upstream * standard).reshape(-1, values.shape[-1]), 0)
    return (grad_values, grad_gain)


def roll_ahead(tile):
    upper_rows = from_behind(tile[:SHIFT], "row", -1)
    rolled = jnp.concatenate([tile[SHIFT:], upper_rows], 0)
    left_cols = from_behind(rolled[:, :SHIFT], "col", -1)
    return jnp.concatenate([rolled[:, SHIFT:], left_cols], 1)


def roll_behind(tile):
    lower_rows = from_behind(tile[-SHIFT:], "row", 1)
    rolled = jnp.concatenate([lower_rows, tile[:-SHIFT]], 0)
    right_cols = from_behind(rolled[:, -SHIFT:], "col", 1)
    return jnp.concatenate([right_cols, rolled[:, :-SHIFT]], 1)


def on_device(features, cotangent, domain, qkv_weight, proj_weight, norm_gain):
    tile_rows, tile_cols, channels = features.shape
    values = features.astype(jnp.float32)
    normed = layer_norm(values, norm_gain).astype(jnp.bfloat16)
    masked_grad = cotangent * domain.astype(jnp.bfloat16)[..., None]
    inside = domain.astype(jnp.float32)[..., None]
    labels = region_labels(
        lax.axis_index("row") * tile_rows,
        tile_rows,
        tile_rows * lax.axis_size("row"),
        lax.axis_index("col") * tile_cols,
        tile_cols,
        tile_cols * lax.axis_size("col"),
    )
    shifted = roll_ahead(normed)
    projected, context, attended = forward_block(shifted, labels, qkv_weight, proj_weight)
    updated = (values + inside * roll_behind(attended).astype(jnp.float32)).astype(jnp.bfloat16)
    dattended = roll_ahead(masked_grad)
    part_qkv, part_proj, dshifted = backward_block(
        shifted, labels, projected, context, dattended, qkv_weight, proj_weight
    )
    dnormed = roll_behind(dshifted)
    grad_values, part_gain = norm_backward(values, norm_gain, dnormed)
    grad_features = (cotangent.astype(jnp.float32) + grad_values).astype(jnp.bfloat16)
    chip_sums = (
        lax.psum(part_qkv.astype(jnp.bfloat16), "col").astype(jnp.float32),
        lax.psum(part_proj.astype(jnp.bfloat16), "col").astype(jnp.float32),
        lax.psum(part_gain.astype(jnp.bfloat16), "col").astype(jnp.float32),
    )
    grad_qkv, grad_proj, grad_gain = lax.psum((chip_sums[0], chip_sums[1], chip_sums[2]), "row")
    return (updated, grad_features, grad_qkv, grad_proj, grad_gain)


def solution(mesh):
    return jax.shard_map(
        on_device,
        mesh=mesh,
        in_specs=(
            P(("grp", "row"), "col", None),
            P(("grp", "row"), "col", None),
            P(("grp", "row"), "col"),
            P(),
            P(),
            P(),
        ),
        out_specs=(
            P(("grp", "row"), "col", None),
            P(("grp", "row"), "col", None),
            P("grp", None),
            P("grp", None),
            P("grp"),
        ),
        check_vma=False,
    )
```

profile of v0, /device:TPU:0, one launch (start us, length us, event | category | flops | bytes accessed | tf_op | source)
XLA Modules:
  0.0 150.2 jit_solution(4569476133203946728)
XLA Ops:
  7.2 0.8 fusion.51
  8.0 1.1 broadcast_multiply_fusion
  9.1 6.0 %collective-permute-start.4 = (bf16[4,64,256]{2,1,0:T(8,128)(2,1)S(1)}, bf16[4,64,256]{2,1,0:T(8,128)(2,1)S(1)}, u32[]{:S(2)}, u32[]{:S(2)}) collective-permute-start(bf16[4,64,256]{2,1,0:T(8,128)(2,1)S(1)} %get-tuple-element.22), channel_id=1, source_target_pairs={{0,14},{2,0},{4,2},{6,4},{8,6},{10,8},{12,10},{14,12},{1,15},{3,1}... | collective-permute-start | bytes 393224 | tf_op jit(solution)/shard_map/ppermute | solution.py:17
  15.1 1.1 convert_reduce_fusion
  16.3 1.2 fusion.24
  17.5 1.2 fusion.22
  19.5 0.8 broadcast_compare_fusion
  20.4 3.3 %collective-permute-done = bf16[4,64,256]{2,1,0:T(8,128)(2,1)S(1)} collective-permute-done((bf16[4,64,256]{2,1,0:T(8,128)(2,1)S(1)}, bf16[4,64,256]{2,1,0:T(8,128)(2,1)S(1)}, u32[]{:S(2)}, u32[]{:S(2)}) %collective-permute-start) | collective-permute-done | bytes 131104 | tf_op jit(solution)/shard_map/ppermute | solution.py:17
  28.3 3.7 %fusion.52 = (f32[8,8,64]{2,1,0:T(8,128)}, f32[8,8,64,64]{2,3,1,0:T(8,128)}) fusion(pred[8,64,64]{1,2,0:T(8,128)(4,1)} %broadcast_compare_fusion, bf16[8,64,8,32]{1,3,2,0:T(8,128)(2,1)S(1)} %bitcast.100, bf16[8,64,8,32]{1,3,2,0:T(8,128)(2,1)S(1)} %bitcast.102), kind=kOutput, calls=%fused_computation.94 | convolution fusion | flops 17825856 | bytes 1622016 | tf_op jit(solution)/shard_map/sub | solution.py:71
  32.1 0.8 multiply_divide_fusion
  32.8 2.3 %fusion.6 = (f32[8,8,64]{2,1,0:T(8,128)S(1)}, bf16[8,8,64,64]{2,3,1,0:T(8,128)(2,1)S(1)}) fusion(f32[8,8,64,64]{2,3,1,0:T(8,128)} %get-tuple-element.30, bf16[8,8,64,64]{2,3,1,0:T(8,128)(2,1)S(1)} %convolution_convert_fusion, f32[8,8,64]{2,1,0:T(8,128)S(1)} %multiply_divide_fusion, f32[8,8,64]{2,1,0:T(8,128)} %get-tuple-element.29), kind=kLoop, calls=%fused_computation.8 | loop fusion | flops 1568768 | bytes 2146304 | tf_op jit(solution)/shard_map/transpose(jvp())/reduce_sum | solution.py:72
  35.2 1.2 fusion.9
  37.1 1.6 %fusion.42 = f32[8,8,64,32]{2,3,1,0:T(8,128)} fusion(bf16[8,64,8,32]{1,3,2,0:T(8,128)(2,1)S(1)} %bitcast.103, f32[8,8,64,64]{2,3,1,0:T(8,128)S(1)} %copy-done.2, bf16[8,8,64,64]{2,3,1,0:T(8,128)(2,1)S(1)} %convolution_convert_fusion, f32[8,8,64]{2,1,0:T(8,128)S(1)} %neg.9, f32[8,8,64]{2,1,0:T(8,128)S(1)} %copy-done.16, pred[8,64,64]{1,2,0:T(8,128)(4,1)S(1)} %copy-done.17), kind=kOutput, calls=%fused_computation.86 | convolution fusion | flops 18350080 | bytes 2424832 | tf_op jit(solution)/shard_map/transpose(jvp(wqhd,wkhd->whqk))/dot_general | solution.py:67
  38.7 1.7 %fusion.44 = f32[8,8,64,32]{2,3,1,0:T(8,128)} fusion(bf16[8,64,8,32]{1,3,2,0:T(8,128)(2,1)S(1)} %bitcast.101, f32[8,8,64,64]{2,3,1,0:T(8,128)S(1)} %copy-done.2, bf16[8,8,64,64]{2,3,1,0:T(8,128)(2,1)S(1)} %convolution_convert_fusion, f32[8,8,64]{2,1,0:T(8,128)S(1)} %neg.9, f32[8,8,64]{2,1,0:T(8,128)S(1)} %copy-done.16, pred[8,64,64]{1,2,0:T(8,128)(4,1)S(1)} %copy-done.17), kind=kOutput, calls=%fused_computation.87 | convolution fusion | flops 18350080 | bytes 2424832 | tf_op jit(solution)/shard_map/transpose(jvp(wqhd,wkhd->whqk))/dot_general | solution.py:67
  40.7 0.9 copy-done.4
  42.0 1.6 %copy.52 = f32[8,64,256]{2,1,0:T(8,128)S(1)} copy(f32[8,64,256]{1,2,0:T(8,128)} %bitcast.94) | data formatting | bytes 1048576 | tf_op jit(solution)/shard_map/transpose(jvp())/reshape | solution.py:64
  43.7 1.1 fusion.8
  45.5 0.7 convert_element_type.151
  47.1 0.9 fusion.10
  48.1 9.6 %collective-permute-done.6 = bf16[4,64,256]{2,1,0:T(8,128)(2,1)S(1)} collective-permute-done((bf16[4,64,256]{2,1,0:T(8,128)(2,1)S(1)}, bf16[4,64,256]{2,1,0:T(8,128)(2,1)S(1)}, u32[]{:S(2)}, u32[]{:S(2)}) %collective-permute-start.6) | collective-permute-done | bytes 131104 | tf_op jit(solution)/shard_map/ppermute | solution.py:17
  59.8 2.5 %psum.46 = bf16[256]{0:T(256)(128)(2,1)S(1)} all-reduce(bf16[256]{0:T(256)(128)(2,1)S(1)} %get-tuple-element.5), channel_id=1, replica_groups=mesh['grp'=2,'row'=8,'col'=2] {'col'}, use_global_device_ids=true, to_apply=%region_12.13 | all-reduce | flops 256 | bytes 1024 | tf_op jit(solution)/shard_map/psum | solution.py:167
  62.3 1.2 add_convert_fusion.1
  63.5 5.5 %all-reduce.8.cloned.1.call-done = (bf16[256,768]{1,0:T(8,128)(2,1)}, bf16[256,256]{1,0:T(8,128)(2,1)}) async-done(((bf16[256,768]{1,0:T(8,128)(2,1)}, bf16[256,256]{1,0:T(8,128)(2,1)}), (bf16[256,768]{1,0:T(8,128)(2,1)}, bf16[256,256]{1,0:T(8,128)(2,1)})) %all-reduce.8.cloned.1.call-update) | async-done | bytes 524304 | tf_op jit(solution)/shard_map/psum | solution.py:165
  69.0 74.4 %all-reduce.9 = (f32[256,768]{1,0:T(8,128)}, f32[256,256]{1,0:T(8,128)}, f32[256]{0:T(256)}) all-reduce(bf16[256,768]{1,0:T(8,128)(2,1)} %get-tuple-element.10, bf16[256,256]{1,0:T(8,128)(2,1)} %get-tuple-element.11, bf16[256]{0:T(256)(128)(2,1)S(1)} %psum.46), channel_id=1, replica_groups=mesh['grp'=2,'row'=8,'col'=2] {'row'}, use_global_device_ids=true, to_apply=%region_8.9 | all-reduce | flops 262400 | bytes 1574400 | tf_op jit(solution)/shard_map/psum | solution.py:169
  (98 shorter events, 10.4 us)
Async XLA Ops:
  7.2 17.8 %copy-start = (bf16[256,768]{1,0:T(8,128)(2,1)S(1)}, bf16[256,768]{1,0:T(8,128)(2,1)}, u32[]{:S(2)}) copy-start(bf16[256,768]{1,0:T(8,128)(2,1)} %param.9) | copy-start | bytes 1179652
  7.2 61.8 %all-reduce.8.cloned.1.call-start = ((), (), s32[]{:S(2)}) async-start(), calls=%async_computation | async-start | bytes 1048576 | tf_op jit(solution)/shard_map/psum | solution.py:165
  9.1 14.9 %copy-start.10 = (bf16[256,256]{1,0:T(8,128)(2,1)S(1)}, bf16[256,256]{1,0:T(8,128)(2,1)}, u32[]{:S(2)}) copy-start(bf16[256,256]{1,0:T(8,128)(2,1)} %param.10) | copy-start | bytes 393220
  9.1 11.2 %collective-permute-start.4 = (bf16[4,64,256]{2,1,0:T(8,128)(2,1)S(1)}, bf16[4,64,256]{2,1,0:T(8,128)(2,1)S(1)}, u32[]{:S(2)}, u32[]{:S(2)}) collective-permute-start(bf16[4,64,256]{2,1,0:T(8,128)(2,1)S(1)} %get-tuple-element.22), channel_id=1, source_target_pairs={{0,14},{2,0},{4,2},{6,4},{8,6},{10,8},{12,10},{14,12},{1,15},{3,1}... | collective-permute-start | bytes 393224 | tf_op jit(solution)/shard_map/ppermute | solution.py:17
  18.7 5.0 %collective-permute-start = (bf16[4,64,256]{2,1,0:T(8,128)(2,1)S(1)}, bf16[4,64,256]{2,1,0:T(8,128)(2,1)S(1)}, u32[]{:S(2)}, u32[]{:S(2)}) collective-permute-start(bf16[4,64,256]{2,1,0:T(8,128)(2,1)S(1)} %get-tuple-element.26), channel_id=1, source_target_pairs={{0,14},{2,0},{4,2},{6,4},{8,6},{10,8},{12,10},{14,12},{1,15},{3,1}... | collective-permute-start | bytes 393224 | tf_op jit(solution)/shard_map/ppermute | solution.py:17
  20.3 3.6 %collective-permute-start.5 = (bf16[8,4,256]{2,1,0:T(4,128)(2,1)S(1)}, bf16[8,4,256]{2,1,0:T(4,128)(2,1)S(1)}, u32[]{:S(2)}, u32[]{:S(2)}) collective-permute-start(bf16[8,4,256]{2,1,0:T(4,128)(2,1)S(1)} %pad_maximum_fusion.5), channel_id=1, source_target_pairs={{0,1},{1,0},{2,3},{3,2},{4,5},{5,4},{6,7},{7,6},{8,9},{9,8},{10,11... | collective-permute-start | bytes 49160 | tf_op jit(solution)/shard_map/ppermute | solution.py:17
  23.7 1.2 collective-permute-start.1
  26.1 2.2 %copy-start.14 = (bf16[8,64,256]{1,2,0:T(8,128)(2,1)}, bf16[8,64,256]{1,2,0:T(8,128)(2,1)S(1)}, u32[]{:S(2)}) copy-start(bf16[8,64,256]{1,2,0:T(8,128)(2,1)S(1)} %copy.39) | copy-start | bytes 786436
  26.4 1.9 %copy-start.12 = (bf16[8,64,256]{1,2,0:T(8,128)(2,1)}, bf16[8,64,256]{1,2,0:T(8,128)(2,1)S(1)}, u32[]{:S(2)}) copy-start(bf16[8,64,256]{1,2,0:T(8,128)(2,1)S(1)} %copy.38) | copy-start | bytes 786436
  35.1 1.9 %copy-start.2 = (f32[8,8,64,64]{2,3,1,0:T(8,128)S(1)}, f32[8,8,64,64]{2,3,1,0:T(8,128)}, u32[]{:S(2)}) copy-start(f32[8,8,64,64]{2,3,1,0:T(8,128)} %get-tuple-element.30) | copy-start | bytes 3145732
  35.1 1.9 %copy-start.15 = (bf16[8,64,256]{1,2,0:T(8,128)(2,1)S(1)}, bf16[8,64,256]{1,2,0:T(8,128)(2,1)}, u32[]{:S(2)}) copy-start(bf16[8,64,256]{1,2,0:T(8,128)(2,1)} %copy-done.14) | copy-start | bytes 786436
  35.1 1.9 %copy-start.16 = (f32[8,8,64]{2,1,0:T(8,128)S(1)}, f32[8,8,64]{2,1,0:T(8,128)}, u32[]{:S(2)}) copy-start(f32[8,8,64]{2,1,0:T(8,128)} %get-tuple-element.29) | copy-start | bytes 49156
  35.1 1.9 %copy-start.17 = (pred[8,64,64]{1,2,0:T(8,128)(4,1)S(1)}, pred[8,64,64]{1,2,0:T(8,128)(4,1)}, u32[]{:S(2)}) copy-start(pred[8,64,64]{1,2,0:T(8,128)(4,1)} %broadcast_compare_fusion) | copy-start | bytes 98308
  37.1 1.6 %copy-start.13 = (bf16[8,64,256]{1,2,0:T(8,128)(2,1)S(1)}, bf16[8,64,256]{1,2,0:T(8,128)(2,1)}, u32[]{:S(2)}) copy-start(bf16[8,64,256]{1,2,0:T(8,128)(2,1)} %copy-done.12) | copy-start | bytes 786436
  40.4 1.2 copy-start.4
  42.0 1.7 %copy-start.9 = (bf16[8,64,256]{2,1,0:T(8,128)(2,1)S(1)}, bf16[8,64,256]{2,1,0:T(8,128)(2,1)}, u32[]{:S(2)}) copy-start(bf16[8,64,256]{2,1,0:T(8,128)(2,1)} %copy-done.8) | copy-start | bytes 786436
  44.9 1.3 copy-start.11
  46.5 12.4 %copy-start.1 = (bf16[8,64,256]{2,1,0:T(8,128)(2,1)S(1)}, bf16[8,64,256]{2,1,0:T(8,128)(2,1)}, u32[]{:S(2)}) copy-start(bf16[8,64,256]{2,1,0:T(8,128)(2,1)} %param.6) | copy-start | bytes 786436
  46.5 12.4 %copy-start.18 = (f32[256]{0:T(256)S(1)}, f32[256]{0:T(256)}, u32[]{:S(2)}) copy-start(f32[256]{0:T(256)} %param.11) | copy-start | bytes 3076
  46.5 11.2 %collective-permute-start.2 = (bf16[4,64,256]{2,1,0:T(8,128)(2,1)S(1)}, bf16[4,64,256]{2,1,0:T(8,128)(2,1)S(1)}, u32[]{:S(2)}, u32[]{:S(2)}) collective-permute-start(bf16[4,64,256]{2,1,0:T(8,128)(2,1)S(1)} %bitcast.104), channel_id=1, source_target_pairs={{0,2},{2,4},{4,6},{6,8},{8,10},{10,12},{12,14},{14,0},{1,3},{3,5},... | collective-permute-start | bytes 393224 | tf_op jit(solution)/shard_map/ppermute | solution.py:17
  47.0 15.3 %copy-start.7 = (bf16[8,64,256]{2,1,0:T(8,128)(2,1)S(1)}, bf16[8,64,256]{2,1,0:T(8,128)(2,1)}, u32[]{:S(2)}) copy-start(bf16[8,64,256]{2,1,0:T(8,128)(2,1)} %param.7) | copy-start | bytes 786436
  47.0 10.6 %collective-permute-start.6 = (bf16[4,64,256]{2,1,0:T(8,128)(2,1)S(1)}, bf16[4,64,256]{2,1,0:T(8,128)(2,1)S(1)}, u32[]{:S(2)}, u32[]{:S(2)}) collective-permute-start(bf16[4,64,256]{2,1,0:T(8,128)(2,1)S(1)} %bitcast.105), channel_id=1, source_target_pairs={{0,2},{2,4},{4,6},{6,8},{8,10},{10,12},{12,14},{14,0},{1,3},{3,5},... | collective-permute-start | bytes 393224 | tf_op jit(solution)/shard_map/ppermute | solution.py:17
  57.7 1.2 collective-permute-start.7
  57.8 4.5 %collective-permute-start.3 = (bf16[8,4,256]{2,1,0:T(4,128)(2,1)S(1)}, bf16[8,4,256]{2,1,0:T(4,128)(2,1)S(1)}, u32[]{:S(2)}, u32[]{:S(2)}) collective-permute-start(bf16[8,4,256]{2,1,0:T(4,128)(2,1)S(1)} %pad_maximum_fusion.6), channel_id=1, source_target_pairs={{0,1},{1,0},{2,3},{3,2},{4,5},{5,4},{6,7},{7,6},{8,9},{9,8},{10,11... | collective-permute-start | bytes 49160 | tf_op jit(solution)/shard_map/ppermute | solution.py:17
  (4 other events, 3.9 us)
Sparse Core Ops, SparseCore 0:
  48.2 20.7 all-reduce.7
where the time goes:
time: 151 us; the launch traced here: 150 us
  blocking collectives  76.8 us (51%)
  waiting for transfers between devices  19.6 us (13%)
  between operations  14.6 us (10%)
  matrix products  12.7 us (8%)
  other arithmetic  11.5 us (8%)
  starting transfers between devices  7.53 us (5%)
  local copies, waits for them, and re-layouts  7.28 us (5%)
    psum x1, blocking collectives, on_device(): lax.psum((chip_sums[0], chip_sums[1], chip_sums[2]), 'row')  74.4 us
    ppermute x8, waiting for transfers between devices, from_behind(): lax.ppermute(array, axis, [(i, (i + by) % peers) for i in range(peers)])  14.1 us
    ppermute x8, starting transfers between devices, from_behind(): lax.ppermute(array, axis, [(i, (i + by) % peers) for i in range(peers)])  7.5 us
    psum x1, waiting for transfers between devices, on_device(): lax.psum(part_qkv.astype(jnp.bfloat16), 'col').astype(jnp.float32)  5.47 us
    sub x1, matrix products, window_core(): weights = jnp.exp(scores - peak)  3.75 us
    dot_general x2, matrix products, window_core(): jnp.einsum('wqhd,wkhd->whqk', query_part, key_part) * head_dim ** (-0.5)  3.33 us
  transfers between devices with their start and end apart: 9, of which 5 were waited for; matrix products, arithmetic and copies ran while one was open for 6% of the time, Pallas kernels for 0%

commit v1 on v0

v1 whole, which is shorter than its diff:
```python
import functools

import jax
import jax.numpy as jnp
from jax import lax
from jax.experimental import pallas as pl
from jax.experimental.pallas import tpu as pltpu
from jax.sharding import PartitionSpec as P

HEADS = 8
WIN = 8
SHIFT = 4
NORM_EPSILON = 1e-05
MASKED_SCORE = -1e30
LOG2E = 1.4426950408889634
INNER = 8
PAD = 16

F32 = jnp.float32
BF16 = jnp.bfloat16


def nn(a, b):
    return lax.dot_general(a, b, (((1,), (0,)), ((), ())), preferred_element_type=F32)


def nt(a, b):
    return lax.dot_general(a, b, (((1,), (1,)), ((), ())), preferred_element_type=F32)


def tn(a, b):
    return lax.dot_general(a, b, (((0,), (0,)), ((), ())), preferred_element_type=F32)


def kernel(
    rows,
    cols,
    feat_ref,
    cot_ref,
    dom_ref,
    wqkv_ref,
    wproj_ref,
    gain_ref,
    upd_ref,
    gfeat_ref,
    gsum_ref,
    ggain_ref,
    ext_f,
    ext_c,
    ext_d,
    xf,
    cf,
    dx,
    mask,
    xhat,
    rstd,
    shifted,
    datt,
    proj,
    dproj,
    ctx,
    dctx,
    out32,
    outx,
    row_in,
    col_in,
    diag_in,
    part,
    core_out,
    core_in,
    gcore_out,
    gcore_in,
    sbuf,
    rbuf,
    obuf,
    oin,
    in_send,
    in_recv,
    out_send,
    out_recv,
    core_send,
    core_recv,
    rs_send,
    rs_recv,
    o_send,
    o_recv,
    ag_send,
    ag_recv,
    fw_send,
    fw_recv,
):
    tile_rows, tile_cols, channels = feat_ref.shape
    windows = tile_cols // WIN
    cells = WIN * WIN
    head_dim = channels // HEADS
    outer = rows // INNER
    me_r = lax.axis_index("row")
    me_c = lax.axis_index("col")
    r_up = lax.rem(me_r + rows - 1, rows)
    r_dn = lax.rem(me_r + 1, rows)
    c_left = lax.rem(me_c + cols - 1, cols)
    c_right = lax.rem(me_c + 1, cols)
    group = me_r // INNER
    member = lax.rem(me_r, INNER)

    def dev(r, c):
        return {"row": r, "col": c}

    def peer(o):
        return group * INNER + lax.rem(member + o, INNER)

    def counterpart(o):
        return lax.rem(group + o, outer) * INNER + member

    barrier = pltpu.get_barrier_semaphore()
    greeted = [
        dev(r_up, me_c),
        dev(r_dn, me_c),
        dev(me_r, c_left),
        dev(r_up, c_left),
        dev(r_dn, c_right),
    ]
    greeted += [dev(peer(o), me_c) for o in range(1, INNER)]
    greeted += [dev(counterpart(o), me_c) for o in range(1, outer)]
    for target in greeted:
        pl.semaphore_signal(barrier, inc=1, device_id=target, device_id_type=pl.DeviceIdType.MESH)
    pl.semaphore_wait(barrier, len(greeted))

    def remote(src, dst, send, recv, target):
        return pltpu.make_async_remote_copy(
            src_ref=src,
            dst_ref=dst,
            send_sem=send,
            recv_sem=recv,
            device_id=target,
            device_id_type=pl.DeviceIdType.MESH,
        )

    up, left, corner = dev(r_up, me_c), dev(me_r, c_left), dev(r_up, c_left)
    top, low = pl.ds(0, SHIFT), pl.ds(SHIFT, SHIFT)
    body, side = pl.ds(0, tile_cols), pl.ds(tile_cols, PAD)
    head = pl.ds(0, PAD)
    jobs = []
    for src, dst in ((feat_ref, ext_f), (cot_ref, ext_c)):
        jobs.append((src.at[top], dst.at[low, body], up))
        jobs.append((src.at[low, head], dst.at[top, side], left))
        jobs.append((src.at[top, head], dst.at[low, side], corner))
    for i, target in enumerate((up, left, corner)):
        jobs.append((dom_ref, ext_d.at[i], target))
    halos = [
        remote(s, d, in_send.at[i], in_recv.at[i], t) for i, (s, d, t) in enumerate(jobs)
    ]
    for copy in halos:
        copy.start()
    out32[:, :, 0:8, :] = jnp.zeros((2, tile_rows, 8, channels), F32)
    out32[:, :, tile_cols : tile_cols + PAD, :] = jnp.zeros((2, tile_rows, PAD, channels), F32)
    xf[0:SHIFT, 0:tile_cols, :] = feat_ref[SHIFT:, :, :].astype(F32)
    cf[0:SHIFT, 0:tile_cols, :] = cot_ref[SHIFT:, :, :].astype(F32)
    for copy in halos:
        copy.wait()
    xf[SHIFT:, 0:tile_cols, :] = ext_f[SHIFT:, 0:tile_cols, :].astype(F32)
    cf[SHIFT:, 0:tile_cols, :] = ext_c[SHIFT:, 0:tile_cols, :].astype(F32)
    xf[:, tile_cols:, :] = ext_f[:, tile_cols:, :].astype(F32)
    cf[:, tile_cols:, :] = ext_c[:, tile_cols:, :].astype(F32)

    lane = lax.broadcasted_iota(jnp.int32, (SHIFT, 2 * tile_cols), 1)
    dx[0:SHIFT, :] = jnp.where(lane < tile_cols, dom_ref[SHIFT:, :], ext_d[1, SHIFT:, :])
    dx[SHIFT:, :] = jnp.where(lane < tile_cols, ext_d[0, 0:SHIFT, :], ext_d[2, 0:SHIFT, :])
    pick = lax.broadcasted_iota(jnp.int32, (WIN, 2 * tile_cols), 1) - lax.broadcasted_iota(
        jnp.int32, (WIN, 2 * tile_cols), 0
    )
    for i in range(tile_rows):
        line = jnp.broadcast_to(dx[i : i + 1, :], (WIN, 2 * tile_cols))
        for w in range(windows):
            mask[w, i * WIN : (i + 1) * WIN, :] = jnp.sum(
                jnp.where(pick == w * WIN + SHIFT, line, 0.0), -1, keepdims=True
            )

    gain = gain_ref[...]
    for w in range(windows):
        at = slice(w * WIN + SHIFT, (w + 1) * WIN + SHIFT)
        x = xf[:, at, :].reshape(cells, channels)
        average = jnp.mean(x, -1, keepdims=True)
        centred = x - average
        variance = jnp.mean(centred * centred, -1, keepdims=True)
        inv = lax.rsqrt(variance + NORM_EPSILON)
        standard = centred * inv
        rstd[w] = inv
        xhat[w] = standard
        shifted[w] = (standard * gain).astype(BF16)
        c = cf[:, at, :].reshape(cells, channels)
        datt[w] = (c * mask[w]).astype(BF16)

    total = windows * cells
    flat_s = shifted[...].reshape(total, channels)
    flat_d = datt[...].reshape(total, channels)
    proj[...] = nn(flat_s, wqkv_ref[...]).astype(BF16).reshape(windows, cells, 3 * channels)
    dctx[...] = nt(flat_d, wproj_ref[...]).astype(BF16).reshape(windows, cells, channels)

    scale = head_dim ** (-0.5)
    half = 128
    per = half // head_dim
    hid = lax.broadcasted_iota(jnp.int32, (per, 1, half), 0)
    lid = lax.broadcasted_iota(jnp.int32, (per, 1, half), 2) // head_dim
    hm32 = jnp.where(hid == lid, 1.0, 0.0).astype(F32)
    hm = hm32.astype(BF16)
    kid = lax.broadcasted_iota(jnp.int32, (cells, cells), 0)
    qid = lax.broadcasted_iota(jnp.int32, (cells, cells), 1)
    mid = WIN * SHIFT
    row_diff = jnp.where((kid >= mid) != (qid >= mid), MASKED_SCORE, 0.0)
    kcol, qcol = lax.rem(kid, WIN) >= SHIFT, lax.rem(qid, WIN) >= SHIFT
    col_diff = jnp.where(kcol != qcol, MASKED_SCORE, 0.0)
    row_bias = row_diff * jnp.where(me_r == rows - 1, 1.0, 0.0)
    last_col = me_c == cols - 1

    def window(w):
        edge = jnp.where(jnp.logical_and(last_col, w == windows - 1), 1.0, 0.0)
        bias = (row_bias + col_diff * edge)[None]
        for t in range(channels // half):
            at = slice(t * half, (t + 1) * half)
            k_at = slice(channels + t * half, channels + (t + 1) * half)
            v_at = slice(2 * channels + t * half, 2 * channels + (t + 1) * half)
            q = proj[w, :, at]
            k = proj[w, :, k_at]
            v = proj[w, :, v_at]
            dc = dctx[w, :, at]
            kx = (k[None] * hm).reshape(per * cells, half)
            vx = (v[None] * hm).reshape(per * cells, half)
            s = nt(kx, q).reshape(per, cells, cells) + bias
            peak = jnp.max(s, 1, keepdims=True)
            e = jnp.exp2((s - peak) * (scale * LOG2E))
            p = e * (1.0 / jnp.sum(e, 1, keepdims=True))
            pb = p.astype(BF16).reshape(per * cells, cells)
            ctx[w, :, at] = tn(pb, vx).astype(BF16)
            dp = nt(vx, dc).astype(BF16).astype(F32).reshape(per, cells, cells)
            ds = p * (dp - jnp.sum(p * dp, 1, keepdims=True))
            dsb = ds.astype(BF16).reshape(per * cells, cells)
            dproj[w, :, at] = (tn(dsb, kx) * scale).astype(BF16)
            dk = nn(dsb, q).reshape(per, cells, half) * hm32
            dproj[w, :, k_at] = (jnp.sum(dk, 0) * scale).astype(BF16)
            dv = nn(pb, dc).reshape(per, cells, half) * hm32
            dproj[w, :, v_at] = jnp.sum(dv, 0).astype(BF16)

    def step(i, carry):
        window(2 * i)
        window(2 * i + 1)
        return carry

    lax.fori_loop(0, windows // 2, step, 0)

    flat_p = dproj[...].reshape(total, 3 * channels)
    flat_c = ctx[...].reshape(total, channels)
    hrows = channels // 2
    part[:, :, 0 : 3 * channels] = tn(flat_s, flat_p).reshape(2, hrows, 3 * channels)
    part[:, :, 3 * channels :] = tn(flat_c, flat_d).reshape(2, hrows, channels)
    other = dev(me_r, c_right)
    core_out[...] = part[c_right].astype(BF16)
    core_copy = remote(core_out, core_in, core_send.at[0], core_recv.at[0], other)
    core_copy.start()

    dnormed = nt(flat_p, wqkv_ref[...]).astype(BF16).astype(F32)
    attended = nn(flat_c, wproj_ref[...]).astype(BF16).astype(F32)
    gsum = jnp.zeros((WIN, channels), F32)
    for w in range(windows):
        at = slice(w * WIN + SHIFT, (w + 1) * WIN + SHIFT)
        dn = dnormed[w * cells : (w + 1) * cells]
        standard = xhat[w]
        gsum = gsum + jnp.sum((dn * standard).reshape(WIN, WIN, channels), 0)
        up_grad = dn * gain
        mean_g = jnp.mean(up_grad, -1, keepdims=True)
        mean_gx = jnp.mean(up_grad * standard, -1, keepdims=True)
        grad = rstd[w] * (up_grad - mean_g - standard * mean_gx)
        out32[1, :, at, :] = cf[:, at, :] + grad.reshape(WIN, WIN, channels)
        inside = mask[w] * attended[w * cells : (w + 1) * cells]
        out32[0, :, at, :] = xf[:, at, :] + inside.reshape(WIN, WIN, channels)
    gtile = jnp.concatenate([gsum[:, :half], gsum[:, half:]], 0)
    gcore_out[...] = gtile.astype(BF16)
    gain_copy = remote(gcore_out, gcore_in, core_send.at[1], core_recv.at[1], other)
    gain_copy.start()
    outx[...] = out32[...].astype(BF16)
    both = pl.ds(0, 2)
    outs = [
        remote(
            outx.at[both, low, body], row_in, out_send.at[0], out_recv.at[0], dev(r_dn, me_c)
        ),
        remote(
            outx.at[both, top, side], col_in, out_send.at[1], out_recv.at[1], dev(me_r, c_right)
        ),
        remote(
            outx.at[both, low, side], diag_in, out_send.at[2], out_recv.at[2], dev(r_dn, c_right)
        ),
    ]

    wide = 4 * channels
    core_copy.wait()
    gain_copy.wait()
    gchip = (gtile + gcore_in[...].astype(F32)).astype(BF16)
    chip = (part[me_c] + core_in[...].astype(F32)).astype(BF16)
    sbuf[:, :, 0:wide] = chip.reshape(INNER, hrows // INNER, wide)
    for j in range(INNER):
        sbuf[j, :, wide:] = gchip
    scatter = [
        remote(
            sbuf.at[lax.rem(member + o, INNER)],
            rbuf.at[o],
            rs_send.at[o],
            rs_recv.at[o],
            dev(peer(o), me_c),
        )
        for o in range(1, INNER)
    ]
    for copy in scatter:
        copy.start()
    for copy in outs:
        copy.start()
    acc = sbuf[member].astype(F32)
    for o in range(1, INNER):
        scatter[o - 1].wait()
        acc = acc + rbuf[o].astype(F32)
    if outer > 1:
        obuf[...] = acc.astype(BF16)
        spread = [
            remote(obuf, oin.at[o], o_send.at[o], o_recv.at[o], dev(counterpart(o), me_c))
            for o in range(1, outer)
        ]
        for copy in spread:
            copy.start()
        for o in range(1, outer):
            spread[o - 1].wait()
            acc = acc + oin[o].astype(F32)

    mine = gsum_ref.at[me_c, member]
    mine[...] = acc[:, 0:wide].astype(BF16)
    gather = [
        remote(mine, mine, ag_send.at[o], ag_recv.at[o], dev(peer(o), me_c))
        for o in range(1, INNER)
    ]
    for copy in gather:
        copy.start()
    forward = [remote(mine, mine, fw_send.at[0], fw_recv.at[0], other)]
    forward[0].start()
    gfold = jnp.concatenate([acc[0:WIN, wide:], acc[WIN:, wide:]], 1)
    ggain_ref[...] = jnp.sum(gfold, 0, keepdims=True)

    for copy in outs:
        copy.wait()
    col_id = lax.broadcasted_iota(jnp.int32, (SHIFT, PAD, channels), 1)
    for n, ref in enumerate((upd_ref, gfeat_ref)):
        ref[0:SHIFT, PAD:, :] = row_in[n, :, PAD:, :]
        ref[SHIFT:, PAD:, :] = outx[n, 0:SHIFT, PAD:tile_cols, :]
        ref[0:SHIFT, 0:PAD, :] = jnp.where(
            col_id < SHIFT, diag_in[n].astype(F32), row_in[n, :, 0:PAD, :].astype(F32)
        ).astype(BF16)
        ref[SHIFT:, 0:PAD, :] = jnp.where(
            col_id < SHIFT, col_in[n].astype(F32), outx[n, 0:SHIFT, 0:PAD, :].astype(F32)
        ).astype(BF16)

    for o in range(1, INNER):
        gather[o - 1].wait()
        piece = gsum_ref.at[me_c, lax.rem(member + INNER - o, INNER)]
        copy = remote(piece, piece, fw_send.at[o], fw_recv.at[o], other)
        copy.start()
        forward.append(copy)
    for copy in forward:
        copy.wait()


def on_device(features, cotangent, domain, qkv_weight, proj_weight, norm_gain):
    tile_rows, tile_cols, channels = features.shape
    rows, cols = lax.axis_size("row"), lax.axis_size("col")
    outer = rows // INNER
    windows, cells = tile_cols // WIN, WIN * WIN
    piece = channels // 2 // INNER
    wide = 4 * channels
    ext = tile_cols + PAD
    vm = pltpu.VMEM
    dma = pltpu.SemaphoreType.DMA
    dom = domain.astype(F32)
    dom = jnp.concatenate([dom, dom], 1)
    vspec = pl.BlockSpec(memory_space=pltpu.VMEM)
    updated, grad_features, gsum, ggain = pl.pallas_call(
        functools.partial(kernel, rows, cols),
        out_shape=(
            jax.ShapeDtypeStruct(features.shape, BF16),
            jax.ShapeDtypeStruct(features.shape, BF16),
            jax.ShapeDtypeStruct((2, INNER, piece, wide), BF16),
            jax.ShapeDtypeStruct((1, channels), F32),
        ),
        in_specs=[vspec] * 6,
        out_specs=(vspec,) * 4,
        scratch_shapes=[
            vm((tile_rows, ext, channels), BF16),
            vm((tile_rows, ext, channels), BF16),
            vm((3, tile_rows, 2 * tile_cols), F32),
            vm((tile_rows, ext, channels), F32),
            vm((tile_rows, ext, channels), F32),
            vm((tile_rows, 2 * tile_cols), F32),
            vm((windows, cells, 1), F32),
            vm((windows, cells, channels), F32),
            vm((windows, cells, 1), F32),
            vm((windows, cells, channels), BF16),
            vm((windows, cells, channels), BF16),
            vm((windows, cells, 3 * channels), BF16),
            vm((windows, cells, 3 * channels), BF16),
            vm((windows, cells, channels), BF16),
            vm((windows, cells, channels), BF16),
            vm((2, tile_rows, ext, channels), F32),
            vm((2, tile_rows, ext, channels), BF16),
            vm((2, SHIFT, tile_cols, channels), BF16),
            vm((2, SHIFT, PAD, channels), BF16),
            vm((2, SHIFT, PAD, channels), BF16),
            vm((2, channels // 2, wide), F32),
            vm((channels // 2, wide), BF16),
            vm((channels // 2, wide), BF16),
            vm((16, 128), BF16),
            vm((16, 128), BF16),
            vm((INNER, piece, wide + 128), BF16),
            vm((INNER, piece, wide + 128), BF16),
            vm((piece, wide + 128), BF16),
            vm((outer, piece, wide + 128), BF16),
            dma((9,)),
            dma((9,)),
            dma((3,)),
            dma((3,)),
            dma((2,)),
            dma((2,)),
            dma((INNER,)),
            dma((INNER,)),
            dma((outer,)),
            dma((outer,)),
            dma((INNER,)),
            dma((INNER,)),
            dma((INNER,)),
            dma((INNER,)),
        ],
        compiler_params=pltpu.CompilerParams(
            collective_id=0, has_side_effects=True, vmem_limit_bytes=48 * 1024 * 1024
        ),
    )(features, cotangent, dom, qkv_weight, proj_weight, norm_gain[None, :])
    sums = gsum.reshape(channels, wide).astype(F32)
    return (
        updated,
        grad_features,
        sums[:, : 3 * channels],
        sums[:, 3 * channels :],
        ggain.reshape(channels),
    )


def solution(mesh):
    return jax.shard_map(
        on_device,
        mesh=mesh,
        in_specs=(
            P(("grp", "row"), "col", None),
            P(("grp", "row"), "col", None),
            P(("grp", "row"), "col"),
            P(),
            P(),
            P(),
        ),
        out_specs=(
            P(("grp", "row"), "col", None),
            P(("grp", "row"), "col", None),
            P("grp", None),
            P("grp", None),
            P("grp"),
        ),
        check_vma=False,
    )
```

time: 151 us -> 59 us (0.39)
  blocking collectives: 76.8 us -> 0 us
  Pallas kernels: 0 us -> 49.1 us
  waiting for transfers between devices: 19.6 us -> 0 us
  between operations: 14.6 us -> 0.66 us
  matrix products: 12.7 us -> 0 us
  other arithmetic: 11.5 us -> 0.9 us
  starting transfers between devices: 7.53 us -> 0 us
    psum x2 -> x0, blocking collectives: 76.8 us -> none  [the longest x1 74.4 us: on_device(): lax.psum((chip_sums[0], chip_sums[1], chip_sums[2]), 'row')]
    pallas_call x0 -> x1, Pallas kernels: none -> 49.1 us  [on_device(): pl.pallas_call(functools.partial(kernel, rows, cols), out_shape=(jax.Shap...]
    ppermute x8 -> x0, waiting for transfers between devices: 14.1 us -> none  [from_behind(): lax.ppermute(array, axis, [(i, (i + by) % peers) for i in range(peers)])]
    dot_general x11 -> x0, matrix products: 9 us -> none  [the longest x2 3.33 us: window_core(): jnp.einsum('wqhd,wkhd->whqk', query_part, key_part) * head_dim ** (-0.5)]
    ppermute x8 -> x0, starting transfers between devices: 7.5 us -> none  [from_behind(): lax.ppermute(array, axis, [(i, (i + by) % peers) for i in range(peers)])]
    psum x1 -> x0, waiting for transfers between devices: 5.47 us -> none  [on_device(): lax.psum(part_qkv.astype(jnp.bfloat16), 'col').astype(jnp.float32)]
    reduce_sum x5 -> x0, other arithmetic: 5.4 us -> none  [the longest x1 2.28 us: window_core(): probability = weights / jnp.sum(weights, -1, keepdims=True)]
    unnamed x38 -> x13, local copies, waits for them, and re-layouts: 1.36 us -> 6.37 us
  transfers between devices with their start and end apart: 9 -> 0, of which waited for: 5 -> 0; matrix products, arithmetic and copies ran while one was open for 6% -> 0% of each run, Pallas kernels for 0% -> 0%
where the time goes in v1:
time: 59 us; the launch traced here: 58.7 us
  Pallas kernels  49.1 us (83%)
  local copies, waits for them, and re-layouts  8.03 us (14%)
  other arithmetic  0.9 us (2%)
  between operations  0.66 us (1%)
    pallas_call x1, Pallas kernels, on_device(): pl.pallas_call(functools.partial(kernel, rows, cols), out_shape=(jax.Shap...  49.1 us
    unnamed x13, local copies, waits for them, and re-layouts  6.37 us

profile of v1, /device:TPU:0, one launch (start us, length us, event | category | flops | bytes accessed | tf_op | source)
XLA Modules:
  0.0 58.7 jit_solution(3471016534535331551)
XLA Ops:
  0.6 0.7 %convert_element_type.9 = f32[8,64]{1,0:T(8,128)S(1)} convert(s32[8,64]{1,0:T(8,128)} %param.8) | non-fusion elementwise | flops 512 | bytes 4096 | tf_op jit(solution)/shard_map/convert_element_type | solution.py:378
  1.3 0.0 copy-start.4
  1.3 0.1 pad_maximum_fusion.dom_ref
  1.4 0.6 %copy-done.4 = f32[256]{0:T(256)S(1)} copy-done((f32[256]{0:T(256)S(1)}, f32[256]{0:T(256)}, u32[]{:S(2)}) %copy-start.4) | copy-done | bytes 1048
  2.0 0.0 copy-start
  2.0 1.0 %copy-done = bf16[256,768]{1,0:T(8,128)(2,1)S(1)} copy-done((bf16[256,768]{1,0:T(8,128)(2,1)S(1)}, bf16[256,768]{1,0:T(8,128)(2,1)}, u32[]{:S(2)}) %copy-start) | copy-done | bytes 393240
  3.0 0.0 copy-start.1
  3.0 0.9 %copy-done.1 = bf16[8,64,256]{2,1,0:T(8,128)(2,1)S(1)} copy-done((bf16[8,64,256]{2,1,0:T(8,128)(2,1)S(1)}, bf16[8,64,256]{2,1,0:T(8,128)(2,1)}, u32[]{:S(2)}) %copy-start.1) | copy-done | bytes 262168
  3.9 0.0 copy-start.2
  3.9 0.9 %copy-done.2 = bf16[8,64,256]{2,1,0:T(8,128)(2,1)S(1)} copy-done((bf16[8,64,256]{2,1,0:T(8,128)(2,1)S(1)}, bf16[8,64,256]{2,1,0:T(8,128)(2,1)}, u32[]{:S(2)}) %copy-start.2) | copy-done | bytes 262168
  4.9 0.0 copy-start.3
  4.9 0.9 %copy-done.3 = bf16[256,256]{1,0:T(8,128)(2,1)S(1)} copy-done((bf16[256,256]{1,0:T(8,128)(2,1)S(1)}, bf16[256,256]{1,0:T(8,128)(2,1)}, u32[]{:S(2)}) %copy-start.3) | copy-done | bytes 131096
  5.8 49.1 %shard_map.101 = (bf16[8,64,256]{2,1,0:T(8,128)(2,1)S(1)}, bf16[8,64,256]{2,1,0:T(8,128)(2,1)S(1)}, bf16[2,8,16,1024]{3,2,1,0:T(8,128)(2,1)S(1)}, f32[1,256]{1,0:T(1,128)S(1)}) custom-call(bf16[8,64,256]{2,1,0:T(8,128)(2,1)S(1)} %copy-done.1, bf16[8,64,256]{2,1,0:T(8,128)(2,1)S(1)} %copy-done.2, f32[8,128]{1,0:T(8,128)S(1)} %pad_maximum_fusion.dom_ref, ...), custom_call_target="tpu_custom_call" | custom-call | tf_op jit(solution)/shard_map/pallas_call | solution.py:381
  54.9 0.1 bitcast_convert_fusion
  55.1 0.7 %slice.9 = f32[256,256]{1,0:T(8,128)} slice(f32[256,1024]{1,0:T(8,128)S(1)} %bitcast_convert_fusion), slice={[0:256], [768:1024]} | slice | bytes 524288 | tf_op jit(solution)/shard_map/slice | solution.py:445
  55.8 0.9 %slice.8 = f32[256,768]{1,0:T(8,128)} slice(f32[256,1024]{1,0:T(8,128)S(1)} %bitcast_convert_fusion), slice={[0:256], [0:768]} | slice | bytes 1572864 | tf_op jit(solution)/shard_map/slice | solution.py:444
  56.7 0.7 %copy.14 = bf16[8,64,256]{2,1,0:T(8,128)(2,1)} copy(bf16[8,64,256]{2,1,0:T(8,128)(2,1)S(1)} %get-tuple-element.18) | data formatting | bytes 524288
  57.4 0.7 %copy.15 = bf16[8,64,256]{2,1,0:T(8,128)(2,1)} copy(bf16[8,64,256]{2,1,0:T(8,128)(2,1)S(1)} %get-tuple-element.19) | data formatting | bytes 524288
  58.1 0.6 copy.16
Async XLA Ops:
  1.3 0.7 %copy-start.4 = (f32[256]{0:T(256)S(1)}, f32[256]{0:T(256)}, u32[]{:S(2)}) copy-start(f32[256]{0:T(256)} %param.11) | copy-start | bytes 3076
  2.0 1.0 %copy-start = (bf16[256,768]{1,0:T(8,128)(2,1)S(1)}, bf16[256,768]{1,0:T(8,128)(2,1)}, u32[]{:S(2)}) copy-start(bf16[256,768]{1,0:T(8,128)(2,1)} %wqkv_ref.1) | copy-start | bytes 1179652
  3.0 0.9 %copy-start.1 = (bf16[8,64,256]{2,1,0:T(8,128)(2,1)S(1)}, bf16[8,64,256]{2,1,0:T(8,128)(2,1)}, u32[]{:S(2)}) copy-start(bf16[8,64,256]{2,1,0:T(8,128)(2,1)} %feat_ref.1) | copy-start | bytes 786436
  3.9 0.9 %copy-start.2 = (bf16[8,64,256]{2,1,0:T(8,128)(2,1)S(1)}, bf16[8,64,256]{2,1,0:T(8,128)(2,1)}, u32[]{:S(2)}) copy-start(bf16[8,64,256]{2,1,0:T(8,128)(2,1)} %cot_ref.1) | copy-start | bytes 786436
  4.9 0.9 %copy-start.3 = (bf16[256,256]{1,0:T(8,128)(2,1)S(1)}, bf16[256,256]{1,0:T(8,128)(2,1)}, u32[]{:S(2)}) copy-start(bf16[256,256]{1,0:T(8,128)(2,1)} %wproj_ref.1) | copy-start | bytes 393220

commit v2 on v1

v2 whole, which is shorter than its diff:
```python
import functools

import jax
import jax.numpy as jnp
from jax import lax
from jax.experimental import pallas as pl
from jax.experimental.pallas import tpu as pltpu
from jax.sharding import PartitionSpec as P

HEADS = 8
WIN = 8
SHIFT = 4
NORM_EPSILON = 1e-05
MASKED_SCORE = -1e30
LOG2E = 1.4426950408889634
INNER = 8
PAD = 16

F32 = jnp.float32
BF16 = jnp.bfloat16


def nn(a, b):
    return lax.dot_general(a, b, (((1,), (0,)), ((), ())), preferred_element_type=F32)


def nt(a, b):
    return lax.dot_general(a, b, (((1,), (1,)), ((), ())), preferred_element_type=F32)


def tn(a, b):
    return lax.dot_general(a, b, (((0,), (0,)), ((), ())), preferred_element_type=F32)


def kernel(
    rows,
    cols,
    feat_hbm,
    cot_hbm,
    dom_hbm,
    wqkv_hbm,
    wproj_hbm,
    gain_hbm,
    upd_hbm,
    gfeat_hbm,
    gsum_hbm,
    ggain_hbm,
    upd_ref,
    gfeat_ref,
    gsum_ref,
    ggain_ref,
    wqkv_ref,
    wproj_ref,
    gain_ref,
    dom_ref,
    dom_out,
    ext_f,
    ext_c,
    ext_d,
    xf,
    cf,
    dx,
    mask,
    xhat,
    rstd,
    shifted,
    datt,
    proj,
    dproj,
    ctx,
    dctx,
    out32,
    outx,
    row_in,
    col_in,
    diag_in,
    own_part,
    core_out,
    core_in,
    gcore_out,
    gcore_in,
    sbuf,
    rbuf,
    obuf,
    oin,
    local_sem,
    done_sem,
    in_send,
    in_recv,
    out_send,
    out_recv,
    core_send,
    core_recv,
    rs_send,
    rs_recv,
    o_send,
    o_recv,
    ag_send,
    ag_recv,
    fw_send,
    fw_recv,
):
    tile_rows, tile_cols, channels = feat_hbm.shape
    windows = tile_cols // WIN
    cells = WIN * WIN
    head_dim = channels // HEADS
    blocks = tile_cols // PAD
    each = PAD // WIN
    outer = rows // INNER
    me_r = lax.axis_index("row")
    me_c = lax.axis_index("col")
    r_up = lax.rem(me_r + rows - 1, rows)
    r_dn = lax.rem(me_r + 1, rows)
    c_left = lax.rem(me_c + cols - 1, cols)
    c_right = lax.rem(me_c + 1, cols)
    group = me_r // INNER
    member = lax.rem(me_r, INNER)

    def dev(r, c):
        return {"row": r, "col": c}

    def peer(o):
        return group * INNER + lax.rem(member + o, INNER)

    def counterpart(o):
        return lax.rem(group + o, outer) * INNER + member

    barrier = pltpu.get_barrier_semaphore()
    greeted = [
        dev(r_up, me_c),
        dev(r_dn, me_c),
        dev(me_r, c_left),
        dev(r_up, c_left),
        dev(r_dn, c_right),
    ]
    greeted += [dev(peer(o), me_c) for o in range(1, INNER)]
    greeted += [dev(counterpart(o), me_c) for o in range(1, outer)]
    for target in greeted:
        pl.semaphore_signal(barrier, inc=1, device_id=target, device_id_type=pl.DeviceIdType.MESH)

    top, low = pl.ds(0, SHIFT), pl.ds(SHIFT, SHIFT)
    body, side, head = pl.ds(0, tile_cols), pl.ds(tile_cols, PAD), pl.ds(0, PAD)
    local = [
        pltpu.make_async_copy(s, d, local_sem.at[i])
        for i, (s, d) in enumerate(
            (
                (dom_hbm, dom_ref),
                (feat_hbm.at[low], ext_f.at[top, body]),
                (cot_hbm.at[low], ext_c.at[top, body]),
                (gain_hbm, gain_ref),
                (wqkv_hbm, wqkv_ref),
                (wproj_hbm, wproj_ref),
            )
        )
    ]
    for copy in local:
        copy.start()
    out32[:, :, 0:8, :] = jnp.zeros((2, tile_rows, 8, channels), F32)
    out32[:, :, tile_cols : tile_cols + PAD, :] = jnp.zeros((2, tile_rows, PAD, channels), F32)
    local[0].wait()
    dom = dom_ref[...].astype(F32)
    dom_out[...] = jnp.concatenate([dom, dom], 1)
    pl.semaphore_wait(barrier, len(greeted))

    def remote(src, dst, send, recv, target):
        return pltpu.make_async_remote_copy(
            src_ref=src,
            dst_ref=dst,
            send_sem=send,
            recv_sem=recv,
            device_id=target,
            device_id_type=pl.DeviceIdType.MESH,
        )

    up, left, corner = dev(r_up, me_c), dev(me_r, c_left), dev(r_up, c_left)
    pairs = ((feat_hbm, ext_f), (cot_hbm, ext_c))
    jobs = [(dom_out, ext_d.at[i], t) for i, t in enumerate((up, left, corner))]
    for b in range(blocks):
        block = pl.ds(b * PAD, PAD)
        jobs += [(s.at[top, block], d.at[low, block], up) for s, d in pairs]
    jobs += [(s.at[low, head], d.at[top, side], left) for s, d in pairs]
    jobs += [(s.at[top, head], d.at[low, side], corner) for s, d in pairs]
    halos = [
        remote(s, d, in_send.at[i], in_recv.at[i], t) for i, (s, d, t) in enumerate(jobs)
    ]
    for copy in halos:
        copy.start()
    for copy in local[1:]:
        copy.wait()
    gain = gain_ref[...]

    scale = head_dim ** (-0.5)
    half = 128
    per = half // head_dim
    hid = lax.broadcasted_iota(jnp.int32, (per, 1, half), 0)
    lid = lax.broadcasted_iota(jnp.int32, (per, 1, half), 2) // head_dim
    hm32 = jnp.where(hid == lid, 1.0, 0.0).astype(F32)
    hm = hm32.astype(BF16)
    kid = lax.broadcasted_iota(jnp.int32, (cells, cells), 0)
    qid = lax.broadcasted_iota(jnp.int32, (cells, cells), 1)
    mid = WIN * SHIFT
    row_diff = jnp.where((kid >= mid) != (qid >= mid), MASKED_SCORE, 0.0)
    kcol, qcol = lax.rem(kid, WIN) >= SHIFT, lax.rem(qid, WIN) >= SHIFT
    col_diff = jnp.where(kcol != qcol, MASKED_SCORE, 0.0)
    row_bias = row_diff * jnp.where(me_r == rows - 1, 1.0, 0.0)
    last_bias = row_bias + col_diff * jnp.where(me_c == cols - 1, 1.0, 0.0)

    for copy in halos[0:3]:
        copy.wait()
    lane = lax.broadcasted_iota(jnp.int32, (SHIFT, 2 * tile_cols), 1)
    dx[0:SHIFT, :] = jnp.where(lane < tile_cols, dom_out[SHIFT:, :], ext_d[1, SHIFT:, :])
    dx[SHIFT:, :] = jnp.where(lane < tile_cols, ext_d[0, 0:SHIFT, :], ext_d[2, 0:SHIFT, :])
    pick = lax.broadcasted_iota(jnp.int32, (WIN, 2 * tile_cols), 1) - lax.broadcasted_iota(
        jnp.int32, (WIN, 2 * tile_cols), 0
    )

    def attend(w):
        bias = (last_bias if w == windows - 1 else row_bias)[None]
        for t in range(channels // half):
            at = slice(t * half, (t + 1) * half)
            k_at = slice(channels + t * half, channels + (t + 1) * half)
            v_at = slice(2 * channels + t * half, 2 * channels + (t + 1) * half)
            q = proj[w, :, at]
            k = proj[w, :, k_at]
            v = proj[w, :, v_at]
            dc = dctx[w, :, at]
            kx = (k[None] * hm).reshape(per * cells, half)
            vx = (v[None] * hm).reshape(per * cells, half)
            s = nt(kx, q).reshape(per, cells, cells) + bias
            peak = jnp.max(s, 1, keepdims=True)
            e = jnp.exp2((s - peak) * (scale * LOG2E))
            p = e * (1.0 / jnp.sum(e, 1, keepdims=True))
            pb = p.astype(BF16).reshape(per * cells, cells)
            ctx[w, :, at] = tn(pb, vx).astype(BF16)
            dp = nt(vx, dc).astype(BF16).astype(F32).reshape(per, cells, cells)
            ds = p * (dp - jnp.sum(p * dp, 1, keepdims=True))
            dsb = ds.astype(BF16).reshape(per * cells, cells)
            dproj[w, :, at] = (tn(dsb, kx) * scale).astype(BF16)
            dk = nn(dsb, q).reshape(per, cells, half) * hm32
            dproj[w, :, k_at] = (jnp.sum(dk, 0) * scale).astype(BF16)
            dv = nn(pb, dc).reshape(per, cells, half) * hm32
            dproj[w, :, v_at] = jnp.sum(dv, 0).astype(BF16)

    gsum = jnp.zeros((WIN, channels), F32)
    both = pl.ds(0, 2)
    outs = []
    for b in range(blocks):
        for n in (0, 1) if b == 0 else (b + 1,):
            first = 3 + 2 * n
            for copy in halos[first : first + (2 if n < blocks else 4)]:
                copy.wait()
            block = slice(n * PAD, (n + 1) * PAD)
            xf[:, block, :] = ext_f[:, block, :].astype(F32)
            cf[:, block, :] = ext_c[:, block, :].astype(F32)
        mine_w = range(b * each, (b + 1) * each)
        for w in mine_w:
            for i in range(tile_rows):
                line = jnp.broadcast_to(dx[i : i + 1, :], (WIN, 2 * tile_cols))
                mask[w, i * WIN : (i + 1) * WIN, :] = jnp.sum(
                    jnp.where(pick == w * WIN + SHIFT, line, 0.0), -1, keepdims=True
                )
            at = slice(w * WIN + SHIFT, (w + 1) * WIN + SHIFT)
            x = xf[:, at, :].reshape(cells, channels)
            average = jnp.mean(x, -1, keepdims=True)
            centred = x - average
            variance = jnp.mean(centred * centred, -1, keepdims=True)
            inv = lax.rsqrt(variance + NORM_EPSILON)
            standard = centred * inv
            rstd[w] = inv
            xhat[w] = standard
            shifted[w] = (standard * gain).astype(BF16)
            c = cf[:, at, :].reshape(cells, channels)
            datt[w] = (c * mask[w]).astype(BF16)
        ws = slice(b * each, (b + 1) * each)
        count = each * cells
        s_chunk = shifted[ws].reshape(count, channels)
        d_chunk = datt[ws].reshape(count, channels)
        proj[ws] = nn(s_chunk, wqkv_ref[...]).astype(BF16).reshape(each, cells, 3 * channels)
        dctx[ws] = nt(d_chunk, wproj_ref[...]).astype(BF16).reshape(each, cells, channels)
        for w in mine_w:
            attend(w)
        p_chunk = dproj[ws].reshape(count, 3 * channels)
        dnormed = nt(p_chunk, wqkv_ref[...]).astype(BF16).astype(F32)
        c_chunk = ctx[ws].reshape(count, channels)
        attended = nn(c_chunk, wproj_ref[...]).astype(BF16).astype(F32)
        for u, w in enumerate(mine_w):
            at = slice(w * WIN + SHIFT, (w + 1) * WIN + SHIFT)
            dn = dnormed[u * cells : (u + 1) * cells]
            standard = xhat[w]
            gsum = gsum + jnp.sum((dn * standard).reshape(WIN, WIN, channels), 0)
            up_grad = dn * gain
            mean_g = jnp.mean(up_grad, -1, keepdims=True)
            mean_gx = jnp.mean(up_grad * standard, -1, keepdims=True)
            grad = rstd[w] * (up_grad - mean_g - standard * mean_gx)
            out32[1, :, at, :] = cf[:, at, :] + grad.reshape(WIN, WIN, channels)
            inside = mask[w] * attended[u * cells : (u + 1) * cells]
            out32[0, :, at, :] = xf[:, at, :] + inside.reshape(WIN, WIN, channels)
        block = slice(b * PAD, (b + 1) * PAD)
        outx[:, :, block, :] = out32[:, :, block, :].astype(BF16)
        area = pl.ds(b * PAD, PAD)
        copy = remote(
            outx.at[both, low, area],
            row_in.at[both, top, area],
            out_send.at[b],
            out_recv.at[b],
            dev(r_dn, me_c),
        )
        copy.start()
        outs.append(copy)

    total = windows * cells
    hrows = channels // 2
    wide = 4 * channels
    other = dev(me_r, c_right)
    flat_p = dproj[...].reshape(total, 3 * channels)
    flat_d = datt[...].reshape(total, channels)

    def half_sum(core):
        at = pl.ds(pl.multiple_of(core * hrows, hrows), hrows)
        left_s = shifted[:, :, at].reshape(total, hrows)
        left_c = ctx[:, :, at].reshape(total, hrows)
        return tn(left_s, flat_p), tn(left_c, flat_d)

    sum_q, sum_p = half_sum(c_right)
    core_out[:, 0 : 3 * channels] = sum_q.astype(BF16)
    core_out[:, 3 * channels :] = sum_p.astype(BF16)
    core_copy = remote(core_out, core_in, core_send.at[0], core_recv.at[0], other)
    core_copy.start()
    gtile = jnp.concatenate([gsum[:, :half], gsum[:, half:]], 0)
    gcore_out[...] = gtile.astype(BF16)
    gain_copy = remote(gcore_out, gcore_in, core_send.at[1], core_recv.at[1], other)
    gain_copy.start()
    sum_q, sum_p = half_sum(me_c)
    own_part[:, 0 : 3 * channels] = sum_q
    own_part[:, 3 * channels :] = sum_p
    edge = slice(tile_cols, tile_cols + PAD)
    outx[:, :, edge, :] = out32[:, :, edge, :].astype(BF16)

    core_copy.wait()
    gain_copy.wait()
    gchip = (gtile + gcore_in[...].astype(F32)).astype(BF16)
    share = hrows // INNER

    def chip_sum(j):
        at = pl.ds(pl.multiple_of(j * share, share), share)
        sbuf[j, :, 0:wide] = (own_part[at, :] + core_in[at, :].astype(F32)).astype(BF16)
        sbuf[j, :, wide:] = gchip

    scatter = [None]
    for o in range(1, INNER):
        j = lax.rem(member + o, INNER)
        chip_sum(j)
        copy = remote(sbuf.at[j], rbuf.at[o], rs_send.at[o], rs_recv.at[o], dev(peer(o), me_c))
        copy.start()
        scatter.append(copy)
    last = [
        remote(
            outx.at[both, top, side],
            col_in,
            out_send.at[blocks],
            out_recv.at[blocks],
            dev(me_r, c_right),
        ),
        remote(
            outx.at[both, low, side],
            diag_in,
            out_send.at[blocks + 1],
            out_recv.at[blocks + 1],
            dev(r_dn, c_right),
        ),
    ]
    for copy in last:
        copy.start()
    outs += last
    chip_sum(member)
    acc = sbuf[member].astype(F32)
    for o in range(1, INNER):
        scatter[o].wait()
        acc = acc + rbuf[o].astype(F32)
    if outer > 1:
        obuf[...] = acc.astype(BF16)
        spread = [
            remote(obuf, oin.at[o], o_send.at[o], o_recv.at[o], dev(counterpart(o), me_c))
            for o in range(1, outer)
        ]
        for copy in spread:
            copy.start()
        for o in range(1, outer):
            spread[o - 1].wait()
            acc = acc + oin[o].astype(F32)

    mine = gsum_ref.at[me_c, member]
    mine[...] = acc[:, 0:wide].astype(BF16)
    gather = [
        remote(mine, mine, ag_send.at[o], ag_recv.at[o], dev(peer(o), me_c))
        for o in range(1, INNER)
    ]
    for copy in gather:
        copy.start()
    forward = [remote(mine, mine, fw_send.at[0], fw_recv.at[0], other)]
    forward[0].start()
    gfold = jnp.concatenate([acc[0:WIN, wide:], acc[WIN:, wide:]], 1)
    ggain_ref[...] = jnp.sum(gfold, 0, keepdims=True)

    def give(i, src, dst):
        copy = pltpu.make_async_copy(src, dst, done_sem.at[i])
        copy.start()
        return copy

    results = [give(0, ggain_ref, ggain_hbm)]
    for copy in outs:
        copy.wait()
    col_id = lax.broadcasted_iota(jnp.int32, (SHIFT, PAD, channels), 1)
    for n, ref in enumerate((upd_ref, gfeat_ref)):
        ref[0:SHIFT, PAD:, :] = row_in[n, :, PAD:, :]
        ref[SHIFT:, PAD:, :] = outx[n, 0:SHIFT, PAD:tile_cols, :]
        ref[0:SHIFT, 0:PAD, :] = jnp.where(
            col_id < SHIFT, diag_in[n].astype(F32), row_in[n, :, 0:PAD, :].astype(F32)
        ).astype(BF16)
        ref[SHIFT:, 0:PAD, :] = jnp.where(
            col_id < SHIFT, col_in[n].astype(F32), outx[n, 0:SHIFT, 0:PAD, :].astype(F32)
        ).astype(BF16)
    results += [give(1, upd_ref, upd_hbm), give(2, gfeat_ref, gfeat_hbm)]

    for o in range(1, INNER):
        gather[o - 1].wait()
        piece = gsum_ref.at[me_c, lax.rem(member + INNER - o, INNER)]
        copy = remote(piece, piece, fw_send.at[o], fw_recv.at[o], other)
        copy.start()
        forward.append(copy)
    results.append(give(3, gsum_ref.at[me_c], gsum_hbm.at[me_c]))
    for copy in forward:
        copy.wait()
    results.append(give(4, gsum_ref.at[c_right], gsum_hbm.at[c_right]))
    for copy in results:
        copy.wait()


def finish(
    upd_in, gfeat_in, gsum_in, ggain_in, upd, gfeat, gqkv, gproj, ggain, sums, qkv32, proj32, sems
):
    channels = gqkv.shape[0]
    halves, _, _, wide = sums.shape
    hrows = channels // halves
    jobs = [(gsum_in.at[c], sums.at[c]) for c in range(halves)]
    jobs += [(upd_in, upd), (gfeat_in, gfeat), (ggain_in, ggain)]
    first = len(jobs)
    for c in range(halves):
        at = pl.ds(c * hrows, hrows)
        jobs += [(proj32.at[at], gproj.at[at]), (qkv32.at[at], gqkv.at[at])]
    copies = [pltpu.make_async_copy(s, d, sems.at[i]) for i, (s, d) in enumerate(jobs)]
    for copy in copies[0:first]:
        copy.start()
    for c in range(halves):
        copies[c].wait()
        at = slice(c * hrows, (c + 1) * hrows)
        some = sums[c].reshape(hrows, wide)
        proj32[at, :] = some[:, 3 * channels :].astype(F32)
        copies[first + 2 * c].start()
        qkv32[at, :] = some[:, : 3 * channels].astype(F32)
        copies[first + 2 * c + 1].start()
    for copy in copies[halves:]:
        copy.wait()


def on_device(features, cotangent, domain, qkv_weight, proj_weight, norm_gain):
    tile_rows, tile_cols, channels = features.shape
    rows, cols = lax.axis_size("row"), lax.axis_size("col")
    outer = rows // INNER
    windows, cells = tile_cols // WIN, WIN * WIN
    blocks = tile_cols // PAD
    piece = channels // 2 // INNER
    wide = 4 * channels
    ext = tile_cols + PAD
    vm = pltpu.VMEM
    dma = pltpu.SemaphoreType.DMA
    halos = 3 + 2 * blocks + 4
    aspec = pl.BlockSpec(memory_space=pltpu.HBM)
    results = pl.pallas_call(
        functools.partial(kernel, rows, cols),
        out_shape=(
            jax.ShapeDtypeStruct(features.shape, BF16),
            jax.ShapeDtypeStruct(features.shape, BF16),
            jax.ShapeDtypeStruct((2, INNER, piece, wide), BF16),
            jax.ShapeDtypeStruct((1, channels), F32),
        ),
        in_specs=[aspec] * 6,
        out_specs=(aspec,) * 4,
        scratch_shapes=[
            vm(features.shape, BF16),
            vm(features.shape, BF16),
            vm((2, INNER, piece, wide), BF16),
            vm((1, channels), F32),
            vm(qkv_weight.shape, BF16),
            vm(proj_weight.shape, BF16),
            vm((1, channels), F32),
            vm((tile_rows, tile_cols), jnp.int32),
            vm((tile_rows, 2 * tile_cols), F32),
            vm((tile_rows, ext, channels), BF16),
            vm((tile_rows, ext, channels), BF16),
            vm((3, tile_rows, 2 * tile_cols), F32),
            vm((tile_rows, ext, channels), F32),
            vm((tile_rows, ext, channels), F32),
            vm((tile_rows, 2 * tile_cols), F32),
            vm((windows, cells, 1), F32),
            vm((windows, cells, channels), F32),
            vm((windows, cells, 1), F32),
            vm((windows, cells, channels), BF16),
            vm((windows, cells, channels), BF16),
            vm((windows, cells, 3 * channels), BF16),
            vm((windows, cells, 3 * channels), BF16),
            vm((windows, cells, channels), BF16),
            vm((windows, cells, channels), BF16),
            vm((2, tile_rows, ext, channels), F32),
            vm((2, tile_rows, ext, channels), BF16),
            vm((2, SHIFT, tile_cols, channels), BF16),
            vm((2, SHIFT, PAD, channels), BF16),
            vm((2, SHIFT, PAD, channels), BF16),
            vm((channels // 2, wide), F32),
            vm((channels // 2, wide), BF16),
            vm((channels // 2, wide), BF16),
            vm((16, 128), BF16),
            vm((16, 128), BF16),
            vm((INNER, piece, wide + 128), BF16),
            vm((INNER, piece, wide + 128), BF16),
            vm((piece, wide + 128), BF16),
            vm((outer, piece, wide + 128), BF16),
            dma((6,)),
            dma((5,)),
            dma((halos,)),
            dma((halos,)),
            dma((blocks + 2,)),
            dma((blocks + 2,)),
            dma((2,)),
            dma((2,)),
            dma((INNER,)),
            dma((INNER,)),
            dma((outer,)),
            dma((outer,)),
            dma((INNER,)),
            dma((INNER,)),
            dma((INNER,)),
            dma((INNER,)),
        ],
        compiler_params=pltpu.CompilerParams(
            collective_id=0, has_side_effects=True, vmem_limit_bytes=60 * 1024 * 1024
        ),
    )(features, cotangent, domain, qkv_weight, proj_weight, norm_gain[None, :])
    outs = pl.pallas_call(
        finish,
        out_shape=(
            jax.ShapeDtypeStruct(features.shape, BF16),
            jax.ShapeDtypeStruct(features.shape, BF16),
            jax.ShapeDtypeStruct((channels, 3 * channels), F32),
            jax.ShapeDtypeStruct((channels, channels), F32),
            jax.ShapeDtypeStruct((1, channels), F32),
        ),
        in_specs=[aspec] * 4,
        out_specs=(aspec,) * 5,
        scratch_shapes=[
            vm((2, INNER, piece, wide), BF16),
            vm((channels, 3 * channels), F32),
            vm((channels, channels), F32),
            dma((9,)),
        ],
        compiler_params=pltpu.CompilerParams(vmem_limit_bytes=60 * 1024 * 1024),
    )(*results)
    return (outs[0], outs[1], outs[2], outs[3], outs[4].reshape(channels))


def solution(mesh):
    return jax.shard_map(
        on_device,
        mesh=mesh,
        in_specs=(
            P(("grp", "row"), "col", None),
            P(("grp", "row"), "col", None),
            P(("grp", "row"), "col"),
            P(),
            P(),
            P(),
        ),
        out_specs=(
            P(("grp", "row"), "col", None),
            P(("grp", "row"), "col", None),
            P("grp", None),
            P("grp", None),
            P("grp"),
        ),
        check_vma=False,
    )
```

time: 59 us -> 60.7 us (1.029)
  Pallas kernels: 49.1 us -> 59.9 us
  local copies, waits for them, and re-layouts: 8.03 us -> 0 us
  other arithmetic: 0.9 us -> 0 us
    pallas_call x0 -> x1, Pallas kernels: none -> 17.1 us  [on_device(): pl.pallas_call(finish, out_shape=(jax.ShapeDtypeStruct(features.shape, BF...]
    unnamed x13 -> x0, local copies, waits for them, and re-layouts: 6.37 us -> none
    pallas_call x1, Pallas kernels: 49.1 us -> 42.8 us  [on_device(): pl.pallas_call(functools.partial(kernel, rows, cols), out_shape=(jax.Shap...]
    slice x2 -> x0, local copies, waits for them, and re-layouts: 1.67 us -> none  [the longest x1 0.94 us: on_device(): sums[:, :3 * channels]]
    convert_element_type x2 -> x0, other arithmetic: 0.83 us -> none  [the longest x1 0.69 us: on_device(): dom = domain.astype(F32)]
where the time goes in v2:
time: 60.7 us; the launch traced here: 60.6 us
  Pallas kernels  59.9 us (99%)
  between operations  0.64 us (1%)
    pallas_call x1, Pallas kernels, on_device(): pl.pallas_call(functools.partial(kernel, rows, cols), out_shape=(jax.Shap...  42.8 us
    pallas_call x1, Pallas kernels, on_device(): pl.pallas_call(finish, out_shape=(jax.ShapeDtypeStruct(features.shape, BF...  17.1 us

profile of v2, /device:TPU:0, one launch (start us, length us, event | category | flops | bytes accessed | tf_op | source)
XLA Modules:
  0.0 60.6 jit_solution(7033136756005031899)
XLA Ops:
  0.6 42.8 %shard_map.101 = (bf16[8,64,256]{2,1,0:T(8,128)(2,1)}, bf16[8,64,256]{2,1,0:T(8,128)(2,1)}, bf16[2,8,16,1024]{3,2,1,0:T(8,128)(2,1)}, f32[1,256]{1,0:T(1,128)}) custom-call(bf16[8,64,256]{2,1,0:T(8,128)(2,1)} %feat_hbm.1, bf16[8,64,256]{2,1,0:T(8,128)(2,1)} %cot_hbm.1, s32[8,64]{1,0:T(8,128)} %dom_hbm.1, bf16[256,768]{1,0:T(8,128)(2,1)} %wqkv_hbm.1, ...), custom_call_target="tpu_custom_call" | custom-call | tf_op jit(solution)/shard_map/pallas_call | solution.py:479
  43.5 17.1 %shard_map.102 = (bf16[8,64,256]{2,1,0:T(8,128)(2,1)}, bf16[8,64,256]{2,1,0:T(8,128)(2,1)}, f32[256,768]{1,0:T(8,128)}, f32[256,256]{1,0:T(8,128)}, f32[1,256]{1,0:T(1,128)}) custom-call(bf16[8,64,256]{2,1,0:T(8,128)(2,1)} %get-tuple-element.14.upd_in, bf16[8,64,256]{2,1,0:T(8,128)(2,1)} %get-tuple-element.15.gfeat_in, ...), custom_call_target="tpu_custom_call" | custom-call | tf_op jit(solution)/shard_map/pallas_call | solution.py:549

commit v3 on v2

--- a/solution.py
+++ b/solution.py
@@ -214,32 +214,31 @@
         jnp.int32, (WIN, 2 * tile_cols), 0
     )
 
-    def attend(w):
+    def attend(w, t):
         bias = (last_bias if w == windows - 1 else row_bias)[None]
-        for t in range(channels // half):
-            at = slice(t * half, (t + 1) * half)
-            k_at = slice(channels + t * half, channels + (t + 1) * half)
-            v_at = slice(2 * channels + t * half, 2 * channels + (t + 1) * half)
-            q = proj[w, :, at]
-            k = proj[w, :, k_at]
-            v = proj[w, :, v_at]
-            dc = dctx[w, :, at]
-            kx = (k[None] * hm).reshape(per * cells, half)
-            vx = (v[None] * hm).reshape(per * cells, half)
-            s = nt(kx, q).reshape(per, cells, cells) + bias
-            peak = jnp.max(s, 1, keepdims=True)
-            e = jnp.exp2((s - peak) * (scale * LOG2E))
-            p = e * (1.0 / jnp.sum(e, 1, keepdims=True))
-            pb = p.astype(BF16).reshape(per * cells, cells)
-            ctx[w, :, at] = tn(pb, vx).astype(BF16)
-            dp = nt(vx, dc).astype(BF16).astype(F32).reshape(per, cells, cells)
-            ds = p * (dp - jnp.sum(p * dp, 1, keepdims=True))
-            dsb = ds.astype(BF16).reshape(per * cells, cells)
-            dproj[w, :, at] = (tn(dsb, kx) * scale).astype(BF16)
-            dk = nn(dsb, q).reshape(per, cells, half) * hm32
-            dproj[w, :, k_at] = (jnp.sum(dk, 0) * scale).astype(BF16)
-            dv = nn(pb, dc).reshape(per, cells, half) * hm32
-            dproj[w, :, v_at] = jnp.sum(dv, 0).astype(BF16)
+        at = slice(t * half, (t + 1) * half)
+        k_at = slice(channels + t * half, channels + (t + 1) * half)
+        v_at = slice(2 * channels + t * half, 2 * channels + (t + 1) * half)
+        q = proj[w, :, at]
+        k = proj[w, :, k_at]
+        v = proj[w, :, v_at]
+        dc = dctx[w, :, at]
+        kx = (k[None] * hm).reshape(per * cells, half)
+        vx = (v[None] * hm).reshape(per * cells, half)
+        s = nt(kx, q).reshape(per, cells, cells) + bias
+        peak = jnp.max(s, 1, keepdims=True)
+        e = jnp.exp2((s - peak) * (scale * LOG2E))
+        p = e * (1.0 / jnp.sum(e, 1, keepdims=True))
+        pb = p.astype(BF16).reshape(per * cells, cells)
+        ctx[w, :, at] = tn(pb, vx).astype(BF16)
+        dp = nt(vx, dc).astype(BF16).astype(F32).reshape(per, cells, cells)
+        ds = p * (dp - jnp.sum(p * dp, 1, keepdims=True))
+        dsb = ds.astype(BF16).reshape(per * cells, cells)
+        dproj[w, :, at] = (tn(dsb, kx) * scale).astype(BF16)
+        dk = nn(dsb, q).reshape(per, cells, half) * hm32
+        dproj[w, :, k_at] = (jnp.sum(dk, 0) * scale).astype(BF16)
+        dv = nn(pb, dc).reshape(per, cells, half) * hm32
+        dproj[w, :, v_at] = jnp.sum(dv, 0).astype(BF16)
 
     gsum = jnp.zeros((WIN, channels), F32)
     both = pl.ds(0, 2)
@@ -278,7 +277,114 @@
         proj[ws] = nn(s_chunk, wqkv_ref[...]).astype(BF16).reshape(each, cells, 3 * channels)
         dctx[ws] = nt(d_chunk, wproj_ref[...]).astype(BF16).reshape(each, cells, channels)
         for w in mine_w:
-            attend(w)
+            attend(w, 0)
+
+    total = windows * cells
+    hrows = channels // 2
+    share = hrows // INNER
+    wide = 4 * half
+    other = dev(me_r, c_right)
+
+    def half_sum(core, t):
+        at = pl.ds(pl.multiple_of(core * hrows, hrows), hrows)
+        left_s = shifted[:, :, at].reshape(total, hrows)
+        right_d = datt[:, :, at].reshape(total, hrows)
+        heads = [
+            dproj[:, :, n * channels + t * half : n * channels + (t + 1) * half].reshape(total, half)
+            for n in range(3)
+        ]
+        left_c = ctx[:, :, t * half : (t + 1) * half].reshape(total, half)
+        return tn(left_s, jnp.concatenate(heads, 1)), tn(left_c, right_d)
+
+    def core_start(t):
+        sum_q, sum_p = half_sum(c_right, t)
+        core_out[t, :, 0 : 3 * half] = sum_q.astype(BF16)
+        core_out[t, :, 3 * half :] = sum_p.astype(BF16)
+        copy = remote(core_out.at[t], core_in.at[t], core_send.at[t], core_recv.at[t], other)
+        copy.start()
+        sum_q, sum_p = half_sum(me_c, t)
+        own_part[t, :, 0 : 3 * half] = sum_q
+        own_part[t, :, 3 * half :] = sum_p
+        return copy
+
+    def chip_sum(j, t, extra):
+        at = pl.ds(pl.multiple_of(j * share, share), share)
+        sbuf[t, j, :, 0:wide] = (own_part[t, at, :] + core_in[t, at, :].astype(F32)).astype(BF16)
+        if extra is not None:
+            sbuf[t, j, :, wide:] = extra
+
+    def span(extra):
+        return pl.ds(0, wide if extra is None else wide + 128)
+
+    def scatter_start(t, extra):
+        copies = [None]
+        for o in range(1, INNER):
+            j = lax.rem(member + o, INNER)
+            chip_sum(j, t, extra)
+            copy = remote(
+                sbuf.at[t, j, :, span(extra)],
+                rbuf.at[t, o, :, span(extra)],
+                rs_send.at[t, o],
+                rs_recv.at[t, o],
+                dev(peer(o), me_c),
+            )
+            copy.start()
+            copies.append(copy)
+        chip_sum(member, t, extra)
+        return copies
+
+    def scatter_end(t, extra, copies):
+        width = wide if extra is None else wide + 128
+        acc = sbuf[t, member, :, 0:width].astype(F32)
+        for o in range(1, INNER):
+            copies[o].wait()
+            acc = acc + rbuf[t, o, :, 0:width].astype(F32)
+        if outer > 1:
+            obuf[t, :, 0:width] = acc.astype(BF16)
+            spread = [
+                remote(
+                    obuf.at[t, :, span(extra)],
+                    oin.at[t, o, :, span(extra)],
+                    o_send.at[t, o],
+                    o_recv.at[t, o],
+                    dev(counterpart(o), me_c),
+                )
+                for o in range(1, outer)
+            ]
+            for copy in spread:
+                copy.start()
+            for o in range(1, outer):
+                spread[o - 1].wait()
+                acc = acc + oin[t, o, :, 0:width].astype(F32)
+        return acc
+
+    def gather_start(t, acc):
+        mine = gsum_ref.at[t, me_c, member]
+        mine[...] = acc[:, 0:wide].astype(BF16)
+        copies = [
+            remote(mine, mine, ag_send.at[t, o], ag_recv.at[t, o], dev(peer(o), me_c))
+            for o in range(1, INNER)
+        ]
+        for copy in copies:
+            copy.start()
+        hand = remote(mine, mine, fw_send.at[t, 0], fw_recv.at[t, 0], other)
+        hand.start()
+        return copies, [hand]
+
+    def gather_end(t, copies, handed):
+        for o in range(1, INNER):
+            copies[o - 1].wait()
+            piece = gsum_ref.at[t, me_c, lax.rem(member + INNER - o, INNER)]
+            copy = remote(piece, piece, fw_send.at[t, o], fw_recv.at[t, o], other)
+            copy.start()
+            handed.append(copy)
+
+    early = core_start(0)
+    for b in range(blocks):
+        ws = slice(b * each, (b + 1) * each)
+        mine_w = range(b * each, (b + 1) * each)
+        for w in mine_w:
+            attend(w, 1)
         p_chunk = dproj[ws].reshape(count, 3 * channels)
         dnormed = nt(p_chunk, wqkv_ref[...]).astype(BF16).astype(F32)
         c_chunk = ctx[ws].reshape(count, channels)
@@ -307,52 +413,23 @@
         )
         copy.start()
         outs.append(copy)
-
-    total = windows * cells
-    hrows = channels // 2
-    wide = 4 * channels
-    other = dev(me_r, c_right)
-    flat_p = dproj[...].reshape(total, 3 * channels)
-    flat_d = datt[...].reshape(total, channels)
-
-    def half_sum(core):
-        at = pl.ds(pl.multiple_of(core * hrows, hrows), hrows)
-        left_s = shifted[:, :, at].reshape(total, hrows)
-        left_c = ctx[:, :, at].reshape(total, hrows)
-        return tn(left_s, flat_p), tn(left_c, flat_d)
-
-    sum_q, sum_p = half_sum(c_right)
-    core_out[:, 0 : 3 * channels] = sum_q.astype(BF16)
-    core_out[:, 3 * channels :] = sum_p.astype(BF16)
-    core_copy = remote(core_out, core_in, core_send.at[0], core_recv.at[0], other)
-    core_copy.start()
+        if b == 0:
+            early.wait()
+            early_scatter = scatter_start(0, None)
+        if b == blocks - 2:
+            early_gather, early_hand = gather_start(0, scatter_end(0, None, early_scatter))
+
+    late = core_start(1)
     gtile = jnp.concatenate([gsum[:, :half], gsum[:, half:]], 0)
     gcore_out[...] = gtile.astype(BF16)
-    gain_copy = remote(gcore_out, gcore_in, core_send.at[1], core_recv.at[1], other)
+    gain_copy = remote(gcore_out, gcore_in, core_send.at[2], core_recv.at[2], other)
     gain_copy.start()
-    sum_q, sum_p = half_sum(me_c)
-    own_part[:, 0 : 3 * channels] = sum_q
-    own_part[:, 3 * channels :] = sum_p
     edge = slice(tile_cols, tile_cols + PAD)
     outx[:, :, edge, :] = out32[:, :, edge, :].astype(BF16)
-
-    core_copy.wait()
+    late.wait()
     gain_copy.wait()
     gchip = (gtile + gcore_in[...].astype(F32)).astype(BF16)
-    share = hrows // INNER
-
-    def chip_sum(j):
-        at = pl.ds(pl.multiple_of(j * share, share), share)
-        sbuf[j, :, 0:wide] = (own_part[at, :] + core_in[at, :].astype(F32)).astype(BF16)
-        sbuf[j, :, wide:] = gchip
-
-    scatter = [None]
-    for o in range(1, INNER):
-        j = lax.rem(member + o, INNER)
-        chip_sum(j)
-        copy = remote(sbuf.at[j], rbuf.at[o], rs_send.at[o], rs_recv.at[o], dev(peer(o), me_c))
-        copy.start()
-        scatter.append(copy)
+    late_scatter = scatter_start(1, gchip)
     last = [
         remote(
             outx.at[both, top, side],
@@ -372,33 +449,9 @@
     for copy in last:
         copy.start()
     outs += last
-    chip_sum(member)
-    acc = sbuf[member].astype(F32)
-    for o in range(1, INNER):
-        scatter[o].wait()
-        acc = acc + rbuf[o].astype(F32)
-    if outer > 1:
-        obuf[...] = acc.astype(BF16)
-        spread = [
-            remote(obuf, oin.at[o], o_send.at[o], o_recv.at[o], dev(counterpart(o), me_c))
-            for o in range(1, outer)
-        ]
-        for copy in spread:
-            copy.start()
-        for o in range(1, outer):
-            spread[o - 1].wait()
-            acc = acc + oin[o].astype(F32)
-
-    mine = gsum_ref.at[me_c, member]
-    mine[...] = acc[:, 0:wide].astype(BF16)
-    gather = [
-        remote(mine, mine, ag_send.at[o], ag_recv.at[o], dev(peer(o), me_c))
-        for o in range(1, INNER)
-    ]
-    for copy in gather:
-        copy.start()
-    forward = [remote(mine, mine, fw_send.at[0], fw_recv.at[0], other)]
-    forward[0].start()
+    gather_end(0, early_gather, early_hand)
+    acc = scatter_end(1, gchip, late_scatter)
+    late_gather, late_hand = gather_start(1, acc)
     gfold = jnp.concatenate([acc[0:WIN, wide:], acc[WIN:, wide:]], 1)
     ggain_ref[...] = jnp.sum(gfold, 0, keepdims=True)
 
@@ -422,44 +475,64 @@
         ).astype(BF16)
     results += [give(1, upd_ref, upd_hbm), give(2, gfeat_ref, gfeat_hbm)]
 
-    for o in range(1, INNER):
-        gather[o - 1].wait()
-        piece = gsum_ref.at[me_c, lax.rem(member + INNER - o, INNER)]
-        copy = remote(piece, piece, fw_send.at[o], fw_recv.at[o], other)
-        copy.start()
-        forward.append(copy)
-    results.append(give(3, gsum_ref.at[me_c], gsum_hbm.at[me_c]))
-    for copy in forward:
+    gather_end(1, late_gather, late_hand)
+    results.append(give(3, gsum_ref.at[both, me_c], gsum_hbm.at[both, me_c]))
+    for copy in early_hand + late_hand:
         copy.wait()
-    results.append(give(4, gsum_ref.at[c_right], gsum_hbm.at[c_right]))
+    results.append(give(4, gsum_ref.at[both, c_right], gsum_hbm.at[both, c_right]))
     for copy in results:
         copy.wait()
 
 
 def finish(
-    upd_in, gfeat_in, gsum_in, ggain_in, upd, gfeat, gqkv, gproj, ggain, sums, qkv32, proj32, sems
+    upd_in,
+    gfeat_in,
+    gsum_in,
+    ggain_in,
+    upd,
+    gfeat,
+    gqkv,
+    gproj,
+    ggain,
+    upd_mid,
+    gfeat_mid,
+    ggain_mid,
+    sums,
+    qkv32,
+    proj32,
+    in_sems,
+    out_sems,
 ):
     channels = gqkv.shape[0]
-    halves, _, _, wide = sums.shape
+    parts, halves, _, _, wide = sums.shape
     hrows = channels // halves
-    jobs = [(gsum_in.at[c], sums.at[c]) for c in range(halves)]
-    jobs += [(upd_in, upd), (gfeat_in, gfeat), (ggain_in, ggain)]
-    first = len(jobs)
-    for c in range(halves):
-        at = pl.ds(c * hrows, hrows)
-        jobs += [(proj32.at[at], gproj.at[at]), (qkv32.at[at], gqkv.at[at])]
-    copies = [pltpu.make_async_copy(s, d, sems.at[i]) for i, (s, d) in enumerate(jobs)]
-    for copy in copies[0:first]:
+    half = wide // 4
+    pairs = [(t, c) for t in range(parts) for c in range(halves)]
+
+    def copies(jobs, sems):
+        return [pltpu.make_async_copy(s, d, sems.at[i]) for i, (s, d) in enumerate(jobs)]
+
+    reads = [(gsum_in.at[t, c], sums.at[t, c]) for t, c in pairs]
+    reads += [(upd_in, upd_mid), (gfeat_in, gfeat_mid), (ggain_in, ggain_mid)]
+    writes = [(qkv32, gqkv), (proj32, gproj)]
+    writes += [(upd_mid, upd), (gfeat_mid, gfeat), (ggain_mid, ggain)]
+    reads, writes = copies(reads, in_sems), copies(writes, out_sems)
+    for copy in reads:
         copy.start()
-    for c in range(halves):
-        copies[c].wait()
-        at = slice(c * hrows, (c + 1) * hrows)
-        some = sums[c].reshape(hrows, wide)
-        proj32[at, :] = some[:, 3 * channels :].astype(F32)
-        copies[first + 2 * c].start()
-        qkv32[at, :] = some[:, : 3 * channels].astype(F32)
-        copies[first + 2 * c + 1].start()
-    for copy in copies[halves:]:
+    for n, (t, c) in enumerate(pairs):
+        reads[n].wait()
+        some = sums[t, c].reshape(hrows, wide).astype(F32)
+        rows = slice(c * hrows, (c + 1) * hrows)
+        for n in range(3):
+            at = slice(n * channels + t * half, n * channels + (t + 1) * half)
+            qkv32[rows, at] = some[:, n * half : (n + 1) * half]
+        proj32[t * half : (t + 1) * half, rows] = some[:, 3 * half :]
+    for n in range(2):
+        writes[n].start()
+    for n in range(3):
+        reads[len(pairs) + n].wait()
+        writes[2 + n].start()
+    for copy in writes:
         copy.wait()
 
 
@@ -470,7 +543,7 @@
     windows, cells = tile_cols // WIN, WIN * WIN
     blocks = tile_cols // PAD
     piece = channels // 2 // INNER
-    wide = 4 * channels
+    wide = 4 * 128
     ext = tile_cols + PAD
     vm = pltpu.VMEM
     dma = pltpu.SemaphoreType.DMA
@@ -481,7 +554,7 @@
         out_shape=(
             jax.ShapeDtypeStruct(features.shape, BF16),
             jax.ShapeDtypeStruct(features.shape, BF16),
-            jax.ShapeDtypeStruct((2, INNER, piece, wide), BF16),
+            jax.ShapeDtypeStruct((2, 2, INNER, piece, wide), BF16),
             jax.ShapeDtypeStruct((1, channels), F32),
         ),
         in_specs=[aspec] * 6,
@@ -489,7 +562,7 @@
         scratch_shapes=[
             vm(features.shape, BF16),
             vm(features.shape, BF16),
-            vm((2, INNER, piece, wide), BF16),
+            vm((2, 2, INNER, piece, wide), BF16),
             vm((1, channels), F32),
             vm(qkv_weight.shape, BF16),
             vm(proj_weight.shape, BF16),
@@ -516,31 +589,31 @@
             vm((2, SHIFT, tile_cols, channels), BF16),
             vm((2, SHIFT, PAD, channels), BF16),
             vm((2, SHIFT, PAD, channels), BF16),
-            vm((channels // 2, wide), F32),
-            vm((channels // 2, wide), BF16),
-            vm((channels // 2, wide), BF16),
+            vm((2, channels // 2, wide), F32),
+            vm((2, channels // 2, wide), BF16),
+            vm((2, channels // 2, wide), BF16),
             vm((16, 128), BF16),
             vm((16, 128), BF16),
-            vm((INNER, piece, wide + 128), BF16),
-            vm((INNER, piece, wide + 128), BF16),
-            vm((piece, wide + 128), BF16),
-            vm((outer, piece, wide + 128), BF16),
+            vm((2, INNER, piece, wide + 128), BF16),
+            vm((2, INNER, piece, wide + 128), BF16),
+            vm((2, piece, wide + 128), BF16),
+            vm((2, outer, piece, wide + 128), BF16),
             dma((6,)),
             dma((5,)),
             dma((halos,)),
             dma((halos,)),
             dma((blocks + 2,)),
             dma((blocks + 2,)),
-            dma((2,)),
-            dma((2,)),
-            dma((INNER,)),
-            dma((INNER,)),
-            dma((outer,)),
-            dma((outer,)),
-            dma((INNER,)),
-            dma((INNER,)),
-            dma((INNER,)),
-            dma((INNER,)),
+            dma((3,)),
+            dma((3,)),
+            dma((2, INNER)),
+            dma((2, INNER)),
+            dma((2, outer)),
+            dma((2, outer)),
+            dma((2, INNER)),
+            dma((2, INNER)),
+            dma((2, INNER)),
+            dma((2, INNER)),
         ],
         compiler_params=pltpu.CompilerParams(
             collective_id=0, has_side_effects=True, vmem_limit_bytes=60 * 1024 * 1024
@@ -558,10 +631,14 @@
         in_specs=[aspec] * 4,
         out_specs=(aspec,) * 5,
         scratch_shapes=[
-            vm((2, INNER, piece, wide), BF16),
+            vm(features.shape, BF16),
+            vm(features.shape, BF16),
+            vm((1, channels), F32),
+            vm((2, 2, INNER, piece, wide), BF16),
             vm((channels, 3 * channels), F32),
             vm((channels, channels), F32),
-            dma((9,)),
+            dma((7,)),
+            dma((5,)),
         ],
         compiler_params=pltpu.CompilerParams(vmem_limit_bytes=60 * 1024 * 1024),
     )(*results)

time: 60.7 us -> 46.7 us (0.77)
  Pallas kernels: 59.9 us -> 45.8 us
    pallas_call x1, Pallas kernels: 17.1 us -> 2.35 us  [on_device(): pl.pallas_call(finish, out_shape=(jax.ShapeDtypeStruct(features.shape, BF...]
    pallas_call x1, Pallas kernels: 42.8 us -> 43.5 us  [on_device(): pl.pallas_call(functools.partial(kernel, rows, cols), out_shape=(jax.Shap...]
where the time goes in v3:
time: 46.7 us; the launch traced here: 46.5 us
  Pallas kernels  45.8 us (98%)
  between operations  0.64 us (1%)
    pallas_call x1, Pallas kernels, on_device(): pl.pallas_call(functools.partial(kernel, rows, cols), out_shape=(jax.Shap...  43.5 us
    pallas_call x1, Pallas kernels, on_device(): pl.pallas_call(finish, out_shape=(jax.ShapeDtypeStruct(features.shape, BF...  2.35 us

profile of v3, /device:TPU:0, one launch (start us, length us, event | category | flops | bytes accessed | tf_op | source)
XLA Modules:
  0.0 46.5 jit_solution(6236673042592595332)
XLA Ops:
  0.6 43.5 %shard_map.101 = (bf16[8,64,256]{2,1,0:T(8,128)(2,1)}, bf16[8,64,256]{2,1,0:T(8,128)(2,1)}, bf16[2,2,8,16,512]{4,3,2,1,0:T(8,128)(2,1)}, f32[1,256]{1,0:T(1,128)}) custom-call(bf16[8,64,256]{2,1,0:T(8,128)(2,1)} %feat_hbm.1, bf16[8,64,256]{2,1,0:T(8,128)(2,1)} %cot_hbm.1, s32[8,64]{1,0:T(8,128)} %dom_hbm.1, bf16[256,768]{1,0:T(8,128)(2,1)} %wqkv_hbm.1, ...), custom_call_target="tpu_custom_call" | custom-call | tf_op jit(solution)/shard_map/pallas_call | solution.py:552
  44.1 2.3 %shard_map.102 = (bf16[8,64,256]{2,1,0:T(8,128)(2,1)}, bf16[8,64,256]{2,1,0:T(8,128)(2,1)}, f32[256,768]{1,0:T(8,128)}, f32[256,256]{1,0:T(8,128)}, f32[1,256]{1,0:T(1,128)}) custom-call(bf16[8,64,256]{2,1,0:T(8,128)(2,1)} %get-tuple-element.14.upd_in, bf16[8,64,256]{2,1,0:T(8,128)(2,1)} %get-tuple-element.15.gfeat_in, ...), custom_call_target="tpu_custom_call" | custom-call | tf_op jit(solution)/shard_map/pallas_call | solution.py:622

commit v4 on v3

--- a/solution.py
+++ b/solution.py
@@ -105,7 +105,9 @@
     cells = WIN * WIN
     head_dim = channels // HEADS
     blocks = tile_cols // PAD
-    each = PAD // WIN
+    chunks = 2
+    each = windows // chunks
+    reach = blocks // chunks
     outer = rows // INNER
     me_r = lax.axis_index("row")
     me_c = lax.axis_index("col")
@@ -214,37 +216,38 @@
         jnp.int32, (WIN, 2 * tile_cols), 0
     )
 
-    def attend(w, t):
-        bias = (last_bias if w == windows - 1 else row_bias)[None]
+    def attend(ws, t):
         at = slice(t * half, (t + 1) * half)
         k_at = slice(channels + t * half, channels + (t + 1) * half)
         v_at = slice(2 * channels + t * half, 2 * channels + (t + 1) * half)
-        q = proj[w, :, at]
-        k = proj[w, :, k_at]
-        v = proj[w, :, v_at]
-        dc = dctx[w, :, at]
-        kx = (k[None] * hm).reshape(per * cells, half)
-        vx = (v[None] * hm).reshape(per * cells, half)
-        s = nt(kx, q).reshape(per, cells, cells) + bias
-        peak = jnp.max(s, 1, keepdims=True)
-        e = jnp.exp2((s - peak) * (scale * LOG2E))
-        p = e * (1.0 / jnp.sum(e, 1, keepdims=True))
-        pb = p.astype(BF16).reshape(per * cells, cells)
-        ctx[w, :, at] = tn(pb, vx).astype(BF16)
-        dp = nt(vx, dc).astype(BF16).astype(F32).reshape(per, cells, cells)
-        ds = p * (dp - jnp.sum(p * dp, 1, keepdims=True))
-        dsb = ds.astype(BF16).reshape(per * cells, cells)
-        dproj[w, :, at] = (tn(dsb, kx) * scale).astype(BF16)
-        dk = nn(dsb, q).reshape(per, cells, half) * hm32
-        dproj[w, :, k_at] = (jnp.sum(dk, 0) * scale).astype(BF16)
-        dv = nn(pb, dc).reshape(per, cells, half) * hm32
-        dproj[w, :, v_at] = jnp.sum(dv, 0).astype(BF16)
+        heads = (per, cells, cells)
+        flat = (per * cells, cells)
+        kx = [(proj[w, :, k_at][None] * hm).reshape(per * cells, half) for w in ws]
+        vx = [(proj[w, :, v_at][None] * hm).reshape(per * cells, half) for w in ws]
+        s = [nt(k, proj[w, :, at]).reshape(heads) for k, w in zip(kx, ws)]
+        dp = [nt(v, dctx[w, :, at]).astype(BF16).astype(F32).reshape(heads) for v, w in zip(vx, ws)]
+        s = [x + (last_bias if w == windows - 1 else row_bias)[None] for x, w in zip(s, ws)]
+        e = [jnp.exp2((x - jnp.max(x, 1, keepdims=True)) * (scale * LOG2E)) for x in s]
+        p = [x * (1.0 / jnp.sum(x, 1, keepdims=True)) for x in e]
+        pb = [x.astype(BF16).reshape(flat) for x in p]
+        ds = [x * (y - jnp.sum(x * y, 1, keepdims=True)) for x, y in zip(p, dp)]
+        dsb = [x.astype(BF16).reshape(flat) for x in ds]
+        for n, w in enumerate(ws):
+            ctx[w, :, at] = tn(pb[n], vx[n]).astype(BF16)
+        for n, w in enumerate(ws):
+            dv = nn(pb[n], dctx[w, :, at]).reshape(per, cells, half) * hm32
+            dproj[w, :, v_at] = jnp.sum(dv, 0).astype(BF16)
+        for n, w in enumerate(ws):
+            dproj[w, :, at] = (tn(dsb[n], kx[n]) * scale).astype(BF16)
+        for n, w in enumerate(ws):
+            dk = nn(dsb[n], proj[w, :, at]).reshape(per, cells, half) * hm32
+            dproj[w, :, k_at] = (jnp.sum(dk, 0) * scale).astype(BF16)
 
     gsum = jnp.zeros((WIN, channels), F32)
     both = pl.ds(0, 2)
     outs = []
-    for b in range(blocks):
-        for n in (0, 1) if b == 0 else (b + 1,):
+    for b in range(chunks):
+        for n in range(b * reach + (b > 0), (b + 1) * reach + 1):
             first = 3 + 2 * n
             for copy in halos[first : first + (2 if n < blocks else 4)]:
                 copy.wait()
@@ -276,8 +279,7 @@
         d_chunk = datt[ws].reshape(count, channels)
         proj[ws] = nn(s_chunk, wqkv_ref[...]).astype(BF16).reshape(each, cells, 3 * channels)
         dctx[ws] = nt(d_chunk, wproj_ref[...]).astype(BF16).reshape(each, cells, channels)
-        for w in mine_w:
-            attend(w, 0)
+        attend(mine_w, 0)
 
     total = windows * cells
     hrows = channels // 2
@@ -380,11 +382,15 @@
             handed.append(copy)
 
     early = core_start(0)
-    for b in range(blocks):
+    for b in range(chunks):
         ws = slice(b * each, (b + 1) * each)
         mine_w = range(b * each, (b + 1) * each)
-        for w in mine_w:
-            attend(w, 1)
+        attend(mine_w, 1)
+        if b == 0:
+            early.wait()
+            early_scatter = scatter_start(0, None)
+        if b == chunks - 1:
+            early_gather, early_hand = gather_start(0, scatter_end(0, None, early_scatter))
         p_chunk = dproj[ws].reshape(count, 3 * channels)
         dnormed = nt(p_chunk, wqkv_ref[...]).astype(BF16).astype(F32)
         c_chunk = ctx[ws].reshape(count, channels)
@@ -401,9 +407,9 @@
             out32[1, :, at, :] = cf[:, at, :] + grad.reshape(WIN, WIN, channels)
             inside = mask[w] * attended[u * cells : (u + 1) * cells]
             out32[0, :, at, :] = xf[:, at, :] + inside.reshape(WIN, WIN, channels)
-        block = slice(b * PAD, (b + 1) * PAD)
+        block = slice(b * reach * PAD, (b + 1) * reach * PAD)
         outx[:, :, block, :] = out32[:, :, block, :].astype(BF16)
-        area = pl.ds(b * PAD, PAD)
+        area = pl.ds(b * reach * PAD, reach * PAD)
         copy = remote(
             outx.at[both, low, area],
             row_in.at[both, top, area],
@@ -413,11 +419,6 @@
         )
         copy.start()
         outs.append(copy)
-        if b == 0:
-            early.wait()
-            early_scatter = scatter_start(0, None)
-        if b == blocks - 2:
-            early_gather, early_hand = gather_start(0, scatter_end(0, None, early_scatter))
 
     late = core_start(1)
     gtile = jnp.concatenate([gsum[:, :half], gsum[:, half:]], 0)

time: 46.7 us -> 47 us (level)
  no operation moved by 1% of the time
where the time goes in v4:
time: 47 us; the launch traced here: 46.8 us
  Pallas kernels  46.1 us (98%)
  between operations  0.64 us (1%)
    pallas_call x1, Pallas kernels, on_device(): pl.pallas_call(functools.partial(kernel, rows, cols), out_shape=(jax.Shap...  43.8 us
    pallas_call x1, Pallas kernels, on_device(): pl.pallas_call(finish, out_shape=(jax.ShapeDtypeStruct(features.shape, BF...  2.35 us

profile of v4, /device:TPU:0, one launch (start us, length us, event | category | flops | bytes accessed | tf_op | source)
XLA Modules:
  0.0 46.8 jit_solution(11160722734767685359)
XLA Ops:
  0.6 43.8 %shard_map.101 = (bf16[8,64,256]{2,1,0:T(8,128)(2,1)}, bf16[8,64,256]{2,1,0:T(8,128)(2,1)}, bf16[2,2,8,16,512]{4,3,2,1,0:T(8,128)(2,1)}, f32[1,256]{1,0:T(1,128)}) custom-call(bf16[8,64,256]{2,1,0:T(8,128)(2,1)} %feat_hbm.1, bf16[8,64,256]{2,1,0:T(8,128)(2,1)} %cot_hbm.1, s32[8,64]{1,0:T(8,128)} %dom_hbm.1, bf16[256,768]{1,0:T(8,128)(2,1)} %wqkv_hbm.1, ...), custom_call_target="tpu_custom_call" | custom-call | tf_op jit(solution)/shard_map/pallas_call | solution.py:553
  44.4 2.3 %shard_map.102 = (bf16[8,64,256]{2,1,0:T(8,128)(2,1)}, bf16[8,64,256]{2,1,0:T(8,128)(2,1)}, f32[256,768]{1,0:T(8,128)}, f32[256,256]{1,0:T(8,128)}, f32[1,256]{1,0:T(1,128)}) custom-call(bf16[8,64,256]{2,1,0:T(8,128)(2,1)} %get-tuple-element.14.upd_in, bf16[8,64,256]{2,1,0:T(8,128)(2,1)} %get-tuple-element.15.gfeat_in, ...), custom_call_target="tpu_custom_call" | custom-call | tf_op jit(solution)/shard_map/pallas_call | solution.py:623

commit v5 on v4

--- a/solution.py
+++ b/solution.py
@@ -54,8 +54,8 @@
     gain_ref,
     dom_ref,
     dom_out,
-    ext_f,
-    ext_c,
+    own,
+    ext,
     ext_d,
     xf,
     cf,
@@ -147,8 +147,8 @@
         for i, (s, d) in enumerate(
             (
                 (dom_hbm, dom_ref),
-                (feat_hbm.at[low], ext_f.at[top, body]),
-                (cot_hbm.at[low], ext_c.at[top, body]),
+                (feat_hbm, own.at[0]),
+                (cot_hbm, own.at[1]),
                 (gain_hbm, gain_ref),
                 (wqkv_hbm, wqkv_ref),
                 (wproj_hbm, wproj_ref),
@@ -162,6 +162,8 @@
     local[0].wait()
     dom = dom_ref[...].astype(F32)
     dom_out[...] = jnp.concatenate([dom, dom], 1)
+    for copy in local[1:3]:
+        copy.wait()
     pl.semaphore_wait(barrier, len(greeted))
 
     def remote(src, dst, send, recv, target):
@@ -175,19 +177,22 @@
         )
 
     up, left, corner = dev(r_up, me_c), dev(me_r, c_left), dev(r_up, c_left)
-    pairs = ((feat_hbm, ext_f), (cot_hbm, ext_c))
+    both = pl.ds(0, 2)
     jobs = [(dom_out, ext_d.at[i], t) for i, t in enumerate((up, left, corner))]
-    for b in range(blocks):
-        block = pl.ds(b * PAD, PAD)
-        jobs += [(s.at[top, block], d.at[low, block], up) for s, d in pairs]
-    jobs += [(s.at[low, head], d.at[top, side], left) for s, d in pairs]
-    jobs += [(s.at[top, head], d.at[low, side], corner) for s, d in pairs]
+    cuts = [0] + [(b * reach + 1) * PAD for b in range(1, chunks)] + [tile_cols]
+    for first, end in zip(cuts, cuts[1:]):
+        area = pl.ds(first, end - first)
+        jobs.append((own.at[both, top, area], ext.at[both, low, area], up))
+    jobs.append((own.at[both, low, head], ext.at[both, top, side], left))
+    jobs.append((own.at[both, top, head], ext.at[both, low, side], corner))
     halos = [
         remote(s, d, in_send.at[i], in_recv.at[i], t) for i, (s, d, t) in enumerate(jobs)
     ]
     for copy in halos:
         copy.start()
-    for copy in local[1:]:
+    xf[0:SHIFT, 0:tile_cols, :] = own[0, SHIFT:, :, :].astype(F32)
+    cf[0:SHIFT, 0:tile_cols, :] = own[1, SHIFT:, :, :].astype(F32)
+    for copy in local[3:]:
         copy.wait()
     gain = gain_ref[...]
 
@@ -244,16 +249,18 @@
             dproj[w, :, k_at] = (jnp.sum(dk, 0) * scale).astype(BF16)
 
     gsum = jnp.zeros((WIN, channels), F32)
-    both = pl.ds(0, 2)
     outs = []
     for b in range(chunks):
-        for n in range(b * reach + (b > 0), (b + 1) * reach + 1):
-            first = 3 + 2 * n
-            for copy in halos[first : first + (2 if n < blocks else 4)]:
+        halos[3 + b].wait()
+        block = slice(cuts[b], cuts[b + 1])
+        xf[SHIFT:, block, :] = ext[0, SHIFT:, block, :].astype(F32)
+        cf[SHIFT:, block, :] = ext[1, SHIFT:, block, :].astype(F32)
+        if b == chunks - 1:
+            for copy in halos[3 + chunks :]:
                 copy.wait()
-            block = slice(n * PAD, (n + 1) * PAD)
-            xf[:, block, :] = ext_f[:, block, :].astype(F32)
-            cf[:, block, :] = ext_c[:, block, :].astype(F32)
+            block = slice(tile_cols, tile_cols + PAD)
+            xf[:, block, :] = ext[0, :, block, :].astype(F32)
+            cf[:, block, :] = ext[1, :, block, :].astype(F32)
         mine_w = range(b * each, (b + 1) * each)
         for w in mine_w:
             for i in range(tile_rows):
@@ -309,44 +316,42 @@
         own_part[t, :, 3 * half :] = sum_p
         return copy
 
-    def chip_sum(j, t, extra):
+    def chip_sum(j, t):
         at = pl.ds(pl.multiple_of(j * share, share), share)
         sbuf[t, j, :, 0:wide] = (own_part[t, at, :] + core_in[t, at, :].astype(F32)).astype(BF16)
-        if extra is not None:
-            sbuf[t, j, :, wide:] = extra
-
-    def span(extra):
-        return pl.ds(0, wide if extra is None else wide + 128)
-
-    def scatter_start(t, extra):
+
+    def scatter_start(t):
         copies = [None]
         for o in range(1, INNER):
             j = lax.rem(member + o, INNER)
-            chip_sum(j, t, extra)
+            chip_sum(j, t)
             copy = remote(
-                sbuf.at[t, j, :, span(extra)],
-                rbuf.at[t, o, :, span(extra)],
+                sbuf.at[t, j],
+                rbuf.at[t, o],
                 rs_send.at[t, o],
                 rs_recv.at[t, o],
                 dev(peer(o), me_c),
             )
             copy.start()
             copies.append(copy)
-        chip_sum(member, t, extra)
+        chip_sum(member, t)
         return copies
 
-    def scatter_end(t, extra, copies):
-        width = wide if extra is None else wide + 128
-        acc = sbuf[t, member, :, 0:width].astype(F32)
+    def scatter_end(t, copies):
+        acc = sbuf[t, member].astype(F32)
         for o in range(1, INNER):
             copies[o].wait()
-            acc = acc + rbuf[t, o, :, 0:width].astype(F32)
+            acc = acc + rbuf[t, o].astype(F32)
+        return acc
+
+    def gather_start(t, acc, extra):
+        acc = jnp.concatenate([acc, extra], 1)
         if outer > 1:
-            obuf[t, :, 0:width] = acc.astype(BF16)
+            obuf[t] = acc.astype(BF16)
             spread = [
                 remote(
-                    obuf.at[t, :, span(extra)],
-                    oin.at[t, o, :, span(extra)],
+                    obuf.at[t],
+                    oin.at[t, o],
                     o_send.at[t, o],
                     o_recv.at[t, o],
                     dev(counterpart(o), me_c),
@@ -357,29 +362,24 @@
                 copy.start()
             for o in range(1, outer):
                 spread[o - 1].wait()
-                acc = acc + oin[t, o, :, 0:width].astype(F32)
-        return acc
-
-    def gather_start(t, acc):
+                acc = acc + oin[t, o].astype(F32)
         mine = gsum_ref.at[t, me_c, member]
-        mine[...] = acc[:, 0:wide].astype(BF16)
+        mine[...] = acc.astype(BF16)
         copies = [
             remote(mine, mine, ag_send.at[t, o], ag_recv.at[t, o], dev(peer(o), me_c))
             for o in range(1, INNER)
         ]
         for copy in copies:
             copy.start()
-        hand = remote(mine, mine, fw_send.at[t, 0], fw_recv.at[t, 0], other)
-        hand.start()
-        return copies, [hand]
-
-    def gather_end(t, copies, handed):
-        for o in range(1, INNER):
-            copies[o - 1].wait()
-            piece = gsum_ref.at[t, me_c, lax.rem(member + INNER - o, INNER)]
-            copy = remote(piece, piece, fw_send.at[t, o], fw_recv.at[t, o], other)
-            copy.start()
-            handed.append(copy)
+        return copies
+
+    def gather_end(t, copies):
+        for copy in copies:
+            copy.wait()
+        column = gsum_ref.at[t, me_c]
+        copy = remote(column, column, fw_send.at[t], fw_recv.at[t], other)
+        copy.start()
+        return copy
 
     early = core_start(0)
     for b in range(chunks):
@@ -388,9 +388,11 @@
         attend(mine_w, 1)
         if b == 0:
             early.wait()
-            early_scatter = scatter_start(0, None)
+            early_scatter = scatter_start(0)
         if b == chunks - 1:
-            early_gather, early_hand = gather_start(0, scatter_end(0, None, early_scatter))
+            acc = scatter_end(0, early_scatter)
+            early_gather = gather_start(0, acc, jnp.zeros((share, 128), F32))
+            late = core_start(1)
         p_chunk = dproj[ws].reshape(count, 3 * channels)
         dnormed = nt(p_chunk, wqkv_ref[...]).astype(BF16).astype(F32)
         c_chunk = ctx[ws].reshape(count, channels)
@@ -420,17 +422,14 @@
         copy.start()
         outs.append(copy)
 
-    late = core_start(1)
+    late.wait()
+    late_scatter = scatter_start(1)
     gtile = jnp.concatenate([gsum[:, :half], gsum[:, half:]], 0)
     gcore_out[...] = gtile.astype(BF16)
     gain_copy = remote(gcore_out, gcore_in, core_send.at[2], core_recv.at[2], other)
     gain_copy.start()
     edge = slice(tile_cols, tile_cols + PAD)
     outx[:, :, edge, :] = out32[:, :, edge, :].astype(BF16)
-    late.wait()
-    gain_copy.wait()
-    gchip = (gtile + gcore_in[...].astype(F32)).astype(BF16)
-    late_scatter = scatter_start(1, gchip)
     last = [
         remote(
             outx.at[both, top, side],
@@ -450,18 +449,17 @@
     for copy in last:
         copy.start()
     outs += last
-    gather_end(0, early_gather, early_hand)
-    acc = scatter_end(1, gchip, late_scatter)
-    late_gather, late_hand = gather_start(1, acc)
-    gfold = jnp.concatenate([acc[0:WIN, wide:], acc[WIN:, wide:]], 1)
-    ggain_ref[...] = jnp.sum(gfold, 0, keepdims=True)
+    early_hand = gather_end(0, early_gather)
+    gain_copy.wait()
+    gchip = gtile + gcore_in[...].astype(F32)
+    late_gather = gather_start(1, scatter_end(1, late_scatter), gchip)
 
     def give(i, src, dst):
         copy = pltpu.make_async_copy(src, dst, done_sem.at[i])
         copy.start()
         return copy
 
-    results = [give(0, ggain_ref, ggain_hbm)]
+    results = []
     for copy in outs:
         copy.wait()
     col_id = lax.broadcasted_iota(jnp.int32, (SHIFT, PAD, channels), 1)
@@ -476,10 +474,14 @@
         ).astype(BF16)
     results += [give(1, upd_ref, upd_hbm), give(2, gfeat_ref, gfeat_hbm)]
 
-    gather_end(1, late_gather, late_hand)
+    late_hand = gather_end(1, late_gather)
     results.append(give(3, gsum_ref.at[both, me_c], gsum_hbm.at[both, me_c]))
-    for copy in early_hand + late_hand:
-        copy.wait()
+    gains = jnp.sum(gsum_ref[1, me_c, :, :, wide:].astype(F32), 0)
+    gfold = jnp.concatenate([gains[0:WIN], gains[WIN:]], 1)
+    ggain_ref[...] = jnp.sum(gfold, 0, keepdims=True)
+    results.append(give(0, ggain_ref, ggain_hbm))
+    early_hand.wait()
+    late_hand.wait()
     results.append(give(4, gsum_ref.at[both, c_right], gsum_hbm.at[both, c_right]))
     for copy in results:
         copy.wait()
@@ -507,7 +509,7 @@
     channels = gqkv.shape[0]
     parts, halves, _, _, wide = sums.shape
     hrows = channels // halves
-    half = wide // 4
+    half = 128
     pairs = [(t, c) for t in range(parts) for c in range(halves)]
 
     def copies(jobs, sems):
@@ -527,7 +529,7 @@
         for n in range(3):
             at = slice(n * channels + t * half, n * channels + (t + 1) * half)
             qkv32[rows, at] = some[:, n * half : (n + 1) * half]
-        proj32[t * half : (t + 1) * half, rows] = some[:, 3 * half :]
+        proj32[t * half : (t + 1) * half, rows] = some[:, 3 * half : 4 * half]
     for n in range(2):
         writes[n].start()
     for n in range(3):
@@ -548,14 +550,14 @@
     ext = tile_cols + PAD
     vm = pltpu.VMEM
     dma = pltpu.SemaphoreType.DMA
-    halos = 3 + 2 * blocks + 4
+    halos = 3 + blocks + 2
     aspec = pl.BlockSpec(memory_space=pltpu.HBM)
     results = pl.pallas_call(
         functools.partial(kernel, rows, cols),
         out_shape=(
             jax.ShapeDtypeStruct(features.shape, BF16),
             jax.ShapeDtypeStruct(features.shape, BF16),
-            jax.ShapeDtypeStruct((2, 2, INNER, piece, wide), BF16),
+            jax.ShapeDtypeStruct((2, 2, INNER, piece, wide + 128), BF16),
             jax.ShapeDtypeStruct((1, channels), F32),
         ),
         in_specs=[aspec] * 6,
@@ -563,15 +565,15 @@
         scratch_shapes=[
             vm(features.shape, BF16),
             vm(features.shape, BF16),
-            vm((2, 2, INNER, piece, wide), BF16),
+            vm((2, 2, INNER, piece, wide + 128), BF16),
             vm((1, channels), F32),
             vm(qkv_weight.shape, BF16),
             vm(proj_weight.shape, BF16),
             vm((1, channels), F32),
             vm((tile_rows, tile_cols), jnp.int32),
             vm((tile_rows, 2 * tile_cols), F32),
-            vm((tile_rows, ext, channels), BF16),
-            vm((tile_rows, ext, channels), BF16),
+            vm((2, tile_rows, tile_cols, channels), BF16),
+            vm((2, tile_rows, ext, channels), BF16),
             vm((3, tile_rows, 2 * tile_cols), F32),
             vm((tile_rows, ext, channels), F32),
             vm((tile_rows, ext, channels), F32),
@@ -595,8 +597,8 @@
             vm((2, channels // 2, wide), BF16),
             vm((16, 128), BF16),
             vm((16, 128), BF16),
-            vm((2, INNER, piece, wide + 128), BF16),
-            vm((2, INNER, piece, wide + 128), BF16),
+            vm((2, INNER, piece, wide), BF16),
+            vm((2, INNER, piece, wide), BF16),
             vm((2, piece, wide + 128), BF16),
             vm((2, outer, piece, wide + 128), BF16),
             dma((6,)),
@@ -613,8 +615,8 @@
             dma((2, outer)),
             dma((2, INNER)),
             dma((2, INNER)),
-            dma((2, INNER)),
-            dma((2, INNER)),
+            dma((2,)),
+            dma((2,)),
         ],
         compiler_params=pltpu.CompilerParams(
             collective_id=0, has_side_effects=True, vmem_limit_bytes=60 * 1024 * 1024
@@ -635,7 +637,7 @@
             vm(features.shape, BF16),
             vm(features.shape, BF16),
             vm((1, channels), F32),
-            vm((2, 2, INNER, piece, wide), BF16),
+            vm((2, 2, INNER, piece, wide + 128), BF16),
             vm((channels, 3 * channels), F32),
             vm((channels, channels), F32),
             dma((7,)),

time: 47 us -> 47.1 us (level)
  no operation moved by 1% of the time
where the time goes in v5:
time: 47.1 us; the launch traced here: 46.9 us
  Pallas kernels  46.2 us (98%)
  between operations  0.64 us (1%)
    pallas_call x1, Pallas kernels, on_device(): pl.pallas_call(functools.partial(kernel, rows, cols), out_shape=(jax.Shap...  43.8 us
    pallas_call x1, Pallas kernels, on_device(): pl.pallas_call(finish, out_shape=(jax.ShapeDtypeStruct(features.shape, BF...  2.41 us

profile of v5, /device:TPU:0, one launch (start us, length us, event | category | flops | bytes accessed | tf_op | source)
XLA Modules:
  0.0 46.9 jit_solution(13512888537181866486)
XLA Ops:
  0.6 43.8 %shard_map.101 = (bf16[8,64,256]{2,1,0:T(8,128)(2,1)}, bf16[8,64,256]{2,1,0:T(8,128)(2,1)}, bf16[2,2,8,16,640]{4,3,2,1,0:T(8,128)(2,1)}, f32[1,256]{1,0:T(1,128)}) custom-call(bf16[8,64,256]{2,1,0:T(8,128)(2,1)} %feat_hbm.1, bf16[8,64,256]{2,1,0:T(8,128)(2,1)} %cot_hbm.1, s32[8,64]{1,0:T(8,128)} %dom_hbm.1, bf16[256,768]{1,0:T(8,128)(2,1)} %wqkv_hbm.1, ...), custom_call_target="tpu_custom_call" | custom-call | tf_op jit(solution)/shard_map/pallas_call | solution.py:555
  44.5 2.4 %shard_map.102 = (bf16[8,64,256]{2,1,0:T(8,128)(2,1)}, bf16[8,64,256]{2,1,0:T(8,128)(2,1)}, f32[256,768]{1,0:T(8,128)}, f32[256,256]{1,0:T(8,128)}, f32[1,256]{1,0:T(1,128)}) custom-call(bf16[8,64,256]{2,1,0:T(8,128)(2,1)} %get-tuple-element.14.upd_in, bf16[8,64,256]{2,1,0:T(8,128)(2,1)} %get-tuple-element.15.gfeat_in, ...), custom_call_target="tpu_custom_call" | custom-call | tf_op jit(solution)/shard_map/pallas_call | solution.py:625

commit v6 on v5

--- a/solution.py
+++ b/solution.py
@@ -73,7 +73,6 @@
     outx,
     row_in,
     col_in,
-    diag_in,
     own_part,
     core_out,
     core_in,
@@ -105,7 +104,7 @@
     cells = WIN * WIN
     head_dim = channels // HEADS
     blocks = tile_cols // PAD
-    chunks = 2
+    chunks = 4
     each = windows // chunks
     reach = blocks // chunks
     outer = rows // INNER
@@ -181,10 +180,10 @@
     jobs = [(dom_out, ext_d.at[i], t) for i, t in enumerate((up, left, corner))]
     cuts = [0] + [(b * reach + 1) * PAD for b in range(1, chunks)] + [tile_cols]
     for first, end in zip(cuts, cuts[1:]):
-        area = pl.ds(first, end - first)
-        jobs.append((own.at[both, top, area], ext.at[both, low, area], up))
+        if first < end:
+            area = pl.ds(first, end - first)
+            jobs.append((own.at[both, top, area], ext.at[both, low, area], up))
     jobs.append((own.at[both, low, head], ext.at[both, top, side], left))
-    jobs.append((own.at[both, top, head], ext.at[both, low, side], corner))
     halos = [
         remote(s, d, in_send.at[i], in_recv.at[i], t) for i, (s, d, t) in enumerate(jobs)
     ]
@@ -251,13 +250,20 @@
     gsum = jnp.zeros((WIN, channels), F32)
     outs = []
     for b in range(chunks):
-        halos[3 + b].wait()
-        block = slice(cuts[b], cuts[b + 1])
-        xf[SHIFT:, block, :] = ext[0, SHIFT:, block, :].astype(F32)
-        cf[SHIFT:, block, :] = ext[1, SHIFT:, block, :].astype(F32)
+        if cuts[b] < cuts[b + 1]:
+            halos[3 + b].wait()
+            block = slice(cuts[b], cuts[b + 1])
+            xf[SHIFT:, block, :] = ext[0, SHIFT:, block, :].astype(F32)
+            cf[SHIFT:, block, :] = ext[1, SHIFT:, block, :].astype(F32)
+        if b == 0:
+            at = len(jobs)
+            passed = remote(
+                ext.at[both, low, head], ext.at[both, low, side], in_send.at[at], in_recv.at[at], left
+            )
+            passed.start()
         if b == chunks - 1:
-            for copy in halos[3 + chunks :]:
-                copy.wait()
+            halos[-1].wait()
+            passed.wait()
             block = slice(tile_cols, tile_cols + PAD)
             xf[:, block, :] = ext[0, :, block, :].astype(F32)
             cf[:, block, :] = ext[1, :, block, :].astype(F32)
@@ -411,44 +417,50 @@
             out32[0, :, at, :] = xf[:, at, :] + inside.reshape(WIN, WIN, channels)
         block = slice(b * reach * PAD, (b + 1) * reach * PAD)
         outx[:, :, block, :] = out32[:, :, block, :].astype(BF16)
-        area = pl.ds(b * reach * PAD, reach * PAD)
-        copy = remote(
-            outx.at[both, low, area],
-            row_in.at[both, top, area],
-            out_send.at[b],
-            out_recv.at[b],
-            dev(r_dn, me_c),
-        )
-        copy.start()
-        outs.append(copy)
-
+        first = max(b * reach, 1) * PAD
+        area = pl.ds(first, (b + 1) * reach * PAD - first)
+        if first < (b + 1) * reach * PAD:
+            copy = remote(
+                outx.at[both, low, area],
+                row_in.at[both, top, area],
+                out_send.at[b],
+                out_recv.at[b],
+                dev(r_dn, me_c),
+            )
+            copy.start()
+            outs.append(copy)
+
+    edge = slice(tile_cols, tile_cols + PAD)
+    outx[:, :, edge, :] = out32[:, :, edge, :].astype(BF16)
+    aside = remote(
+        outx.at[both, pl.ds(0, tile_rows), side],
+        col_in,
+        out_send.at[blocks],
+        out_recv.at[blocks],
+        dev(me_r, c_right),
+    )
+    aside.start()
     late.wait()
     late_scatter = scatter_start(1)
     gtile = jnp.concatenate([gsum[:, :half], gsum[:, half:]], 0)
     gcore_out[...] = gtile.astype(BF16)
     gain_copy = remote(gcore_out, gcore_in, core_send.at[2], core_recv.at[2], other)
     gain_copy.start()
-    edge = slice(tile_cols, tile_cols + PAD)
-    outx[:, :, edge, :] = out32[:, :, edge, :].astype(BF16)
-    last = [
-        remote(
-            outx.at[both, top, side],
-            col_in,
-            out_send.at[blocks],
-            out_recv.at[blocks],
-            dev(me_r, c_right),
-        ),
-        remote(
-            outx.at[both, low, side],
-            diag_in,
-            out_send.at[blocks + 1],
-            out_recv.at[blocks + 1],
-            dev(r_dn, c_right),
-        ),
-    ]
-    for copy in last:
-        copy.start()
-    outs += last
+    aside.wait()
+    col_id = lax.broadcasted_iota(jnp.int32, (tile_rows, PAD, channels), 1)
+    for n in range(2):
+        outx[n, :, 0:PAD, :] = jnp.where(
+            col_id < SHIFT, col_in[n].astype(F32), outx[n, :, 0:PAD, :].astype(F32)
+        ).astype(BF16)
+    copy = remote(
+        outx.at[both, low, head],
+        row_in.at[both, top, head],
+        out_send.at[blocks + 1],
+        out_recv.at[blocks + 1],
+        dev(r_dn, me_c),
+    )
+    copy.start()
+    outs.append(copy)
     early_hand = gather_end(0, early_gather)
     gain_copy.wait()
     gchip = gtile + gcore_in[...].astype(F32)
@@ -462,16 +474,9 @@
     results = []
     for copy in outs:
         copy.wait()
-    col_id = lax.broadcasted_iota(jnp.int32, (SHIFT, PAD, channels), 1)
     for n, ref in enumerate((upd_ref, gfeat_ref)):
-        ref[0:SHIFT, PAD:, :] = row_in[n, :, PAD:, :]
-        ref[SHIFT:, PAD:, :] = outx[n, 0:SHIFT, PAD:tile_cols, :]
-        ref[0:SHIFT, 0:PAD, :] = jnp.where(
-            col_id < SHIFT, diag_in[n].astype(F32), row_in[n, :, 0:PAD, :].astype(F32)
-        ).astype(BF16)
-        ref[SHIFT:, 0:PAD, :] = jnp.where(
-            col_id < SHIFT, col_in[n].astype(F32), outx[n, 0:SHIFT, 0:PAD, :].astype(F32)
-        ).astype(BF16)
+        ref[0:SHIFT, :, :] = row_in[n]
+        ref[SHIFT:, :, :] = outx[n, 0:SHIFT, 0:tile_cols, :]
     results += [give(1, upd_ref, upd_hbm), give(2, gfeat_ref, gfeat_hbm)]
 
     late_hand = gather_end(1, late_gather)
@@ -590,8 +595,7 @@
             vm((2, tile_rows, ext, channels), F32),
             vm((2, tile_rows, ext, channels), BF16),
             vm((2, SHIFT, tile_cols, channels), BF16),
-            vm((2, SHIFT, PAD, channels), BF16),
-            vm((2, SHIFT, PAD, channels), BF16),
+            vm((2, tile_rows, PAD, channels), BF16),
             vm((2, channels // 2, wide), F32),
             vm((2, channels // 2, wide), BF16),
             vm((2, channels // 2, wide), BF16),

time: 47.1 us -> 45.6 us (0.968)
  Pallas kernels: 46.2 us -> 44.8 us
    pallas_call x1, Pallas kernels: 43.8 us -> 42.4 us  [on_device(): pl.pallas_call(functools.partial(kernel, rows, cols), out_shape=(jax.Shap...]
where the time goes in v6:
time: 45.6 us; the launch traced here: 45.4 us
  Pallas kernels  44.8 us (98%)
  between operations  0.64 us (1%)
    pallas_call x1, Pallas kernels, on_device(): pl.pallas_call(functools.partial(kernel, rows, cols), out_shape=(jax.Shap...  42.4 us
    pallas_call x1, Pallas kernels, on_device(): pl.pallas_call(finish, out_shape=(jax.ShapeDtypeStruct(features.shape, BF...  2.41 us

profile of v6, /device:TPU:0, one launch (start us, length us, event | category | flops | bytes accessed | tf_op | source)
XLA Modules:
  0.0 45.4 jit_solution(11262108735354354969)
XLA Ops:
  0.6 42.4 %shard_map.101 = (bf16[8,64,256]{2,1,0:T(8,128)(2,1)}, bf16[8,64,256]{2,1,0:T(8,128)(2,1)}, bf16[2,2,8,16,640]{4,3,2,1,0:T(8,128)(2,1)}, f32[1,256]{1,0:T(1,128)}) custom-call(bf16[8,64,256]{2,1,0:T(8,128)(2,1)} %feat_hbm.1, bf16[8,64,256]{2,1,0:T(8,128)(2,1)} %cot_hbm.1, s32[8,64]{1,0:T(8,128)} %dom_hbm.1, bf16[256,768]{1,0:T(8,128)(2,1)} %wqkv_hbm.1, ...), custom_call_target="tpu_custom_call" | custom-call | tf_op jit(solution)/shard_map/pallas_call | solution.py:560
  43.0 2.4 %shard_map.102 = (bf16[8,64,256]{2,1,0:T(8,128)(2,1)}, bf16[8,64,256]{2,1,0:T(8,128)(2,1)}, f32[256,768]{1,0:T(8,128)}, f32[256,256]{1,0:T(8,128)}, f32[1,256]{1,0:T(1,128)}) custom-call(bf16[8,64,256]{2,1,0:T(8,128)(2,1)} %get-tuple-element.14.upd_in, bf16[8,64,256]{2,1,0:T(8,128)(2,1)} %get-tuple-element.15.gfeat_in, ...), custom_call_target="tpu_custom_call" | custom-call | tf_op jit(solution)/shard_map/pallas_call | solution.py:629

commit v7 on v6

--- a/solution.py
+++ b/solution.py
@@ -395,9 +395,10 @@
         if b == 0:
             early.wait()
             early_scatter = scatter_start(0)
-        if b == chunks - 1:
+        if b == chunks - 2:
             acc = scatter_end(0, early_scatter)
             early_gather = gather_start(0, acc, jnp.zeros((share, 128), F32))
+        if b == chunks - 1:
             late = core_start(1)
         p_chunk = dproj[ws].reshape(count, 3 * channels)
         dnormed = nt(p_chunk, wqkv_ref[...]).astype(BF16).astype(F32)

time: 45.6 us -> 45.7 us (level)
  no operation moved by 1% of the time
where the time goes in v7:
time: 45.7 us; the launch traced here: 45.5 us
  Pallas kernels  44.9 us (98%)
  between operations  0.64 us (1%)
    pallas_call x1, Pallas kernels, on_device(): pl.pallas_call(functools.partial(kernel, rows, cols), out_shape=(jax.Shap...  42.5 us
    pallas_call x1, Pallas kernels, on_device(): pl.pallas_call(finish, out_shape=(jax.ShapeDtypeStruct(features.shape, BF...  2.41 us

profile of v7, /device:TPU:0, one launch (start us, length us, event | category | flops | bytes accessed | tf_op | source)
XLA Modules:
  0.0 45.5 jit_solution(14128238327689844433)
XLA Ops:
  0.6 42.5 %shard_map.101 = (bf16[8,64,256]{2,1,0:T(8,128)(2,1)}, bf16[8,64,256]{2,1,0:T(8,128)(2,1)}, bf16[2,2,8,16,640]{4,3,2,1,0:T(8,128)(2,1)}, f32[1,256]{1,0:T(1,128)}) custom-call(bf16[8,64,256]{2,1,0:T(8,128)(2,1)} %feat_hbm.1, bf16[8,64,256]{2,1,0:T(8,128)(2,1)} %cot_hbm.1, s32[8,64]{1,0:T(8,128)} %dom_hbm.1, bf16[256,768]{1,0:T(8,128)(2,1)} %wqkv_hbm.1, ...), custom_call_target="tpu_custom_call" | custom-call | tf_op jit(solution)/shard_map/pallas_call | solution.py:561
  43.1 2.4 %shard_map.102 = (bf16[8,64,256]{2,1,0:T(8,128)(2,1)}, bf16[8,64,256]{2,1,0:T(8,128)(2,1)}, f32[256,768]{1,0:T(8,128)}, f32[256,256]{1,0:T(8,128)}, f32[1,256]{1,0:T(1,128)}) custom-call(bf16[8,64,256]{2,1,0:T(8,128)(2,1)} %get-tuple-element.14.upd_in, bf16[8,64,256]{2,1,0:T(8,128)(2,1)} %get-tuple-element.15.gfeat_in, ...), custom_call_target="tpu_custom_call" | custom-call | tf_op jit(solution)/shard_map/pallas_call | solution.py:630
